TPU v7x, 128 devices: a whole 4x4x4 slice. The times are simulated.
128 devices in a mesh: dp: 16 (over z, x_lo, core), tensor: 8 (over y, x_hi).
Axes of the slice: x: 4 (x_hi: 2, x_lo: 2; x = x_hi * 2 + x_lo), y: 4, z: 4, core: 2. Of those that a mesh axis runs over, the one named last changes fastest.
Arguments:
- tokens: bfloat16 [20480, 2048], P(('dp', 'tensor')), may hold values from -6 to 6
- lengths: int32 [16, 3], P('dp'), may hold values from 1 to 1024, 1280 in all within a row
- order: int32 [16, 1280], P('dp'), may hold values from 0 to 1279, each once within a row
- sequence_adapter: int32 [16, 3], P('dp'), may hold values from 0 to 7
- first_norm_gain: float32 [1, 2048], replicated, may hold values from 0.5 to 1.5
- first_norm_bias: float32 [1, 2048], replicated, may hold values from -4 to 4
- second_norm_gain: float32 [1, 2048], replicated, may hold values from 0.5 to 1.5
- second_norm_bias: float32 [1, 2048], replicated, may hold values from -4 to 4
- joined_matrix: bfloat16 [1, 2048, 6144], P(None, 'dp', 'tensor'), may hold values from -0.125 to 0.125
- joined_offset_bias: float32 [1, 6144], P(None, 'tensor'), may hold values from -4 to 4
- output_matrix: bfloat16 [1, 2048, 2048], P(None, 'tensor', 'dp'), may hold values from -0.25 to 0.25
- output_offset_bias: float32 [1, 2048], replicated, may hold values from -4 to 4
- up_matrix: bfloat16 [1, 2048, 8192], P(None, 'dp', 'tensor'), may hold values from -0.125 to 0.125
- up_offset_bias: float32 [1, 8192], P(None, 'tensor'), may hold values from -4 to 4
- down_matrix: bfloat16 [1, 8192, 2048], P(None, 'tensor', 'dp'), may hold values from -0.09375 to 0.09375
- down_offset_bias: float32 [1, 2048], replicated, may hold values from -4 to 4
- joined_adapter_reduce: bfloat16 [1, 2048, 128], replicated, may hold values from -0.125 to 0.125
- joined_adapter_expand: bfloat16 [1, 128, 6144], P(None, None, 'tensor'), may hold values from -1.5 to 1.5
- output_adapter_reduce: bfloat16 [1, 2048, 128], P(None, 'tensor'), may hold values from -0.25 to 0.25
- output_adapter_expand: bfloat16 [1, 128, 2048], replicated, may hold values from -1.5 to 1.5
- up_adapter_reduce: bfloat16 [1, 2048, 128], replicated, may hold values from -0.125 to 0.125
- up_adapter_expand: bfloat16 [1, 128, 8192], P(None, None, 'tensor'), may hold values from -1.5 to 1.5
- down_adapter_reduce: bfloat16 [1, 8192, 128], P(None, 'tensor'), may hold values from -0.09375 to 0.09375
- down_adapter_expand: bfloat16 [1, 128, 2048], replicated, may hold values from -1.5 to 1.5
- cotangent: bfloat16 [20480, 2048], P(('dp', 'tensor')), may hold values from -6 to 6
Outputs:
- block_out: float32 [20480, 2048], P(('dp', 'tensor'))
- input_grad: float32 [20480, 2048], P(('dp', 'tensor'))
- qkv_lora_a_grad: float32 [1, 2048, 128], replicated
- qkv_lora_b_grad: float32 [1, 128, 6144], P(None, None, 'tensor')
- out_lora_a_grad: float32 [1, 2048, 128], P(None, 'tensor')
- out_lora_b_grad: float32 [1, 128, 2048], replicated
- up_lora_a_grad: float32 [1, 2048, 128], replicated
- up_lora_b_grad: float32 [1, 128, 8192], P(None, None, 'tensor')
- down_lora_a_grad: float32 [1, 8192, 128], P(None, 'tensor')
- down_lora_b_grad: float32 [1, 128, 2048], replicated
Inputs may be any that keep to these rules, and one draw needn't show every extreme that they name: `order`: each row holds every number of 0 to 1279 once.
All inputs are finite; a program needn't handle non-finite values.
Results may differ from a plain program's by a relative error of at most 0.02.
Values may be sent and summed in bfloat16 or wider, within the bound.
A program may use at most 128 MiB of HBM per device.

v0:
```python
import functools
import math

import jax
import jax.numpy as jnp
from jax import lax
from jax.experimental import pallas as pl
from jax.experimental.pallas import tpu as pltpu
from jax.sharding import PartitionSpec as P

HEAD = 128
WIDTH = 2048
LANES = 128
WIDE = WIDTH + LANES
ROWS = 160
HALF = ROWS // 2
PAIR = 2 * ROWS
GROUP = 8 * ROWS
QKV = 768
UNITS = 1024
CTX = 256
BLOCK = 32
SCALE = 0.5
EPS = 1e-05
MASKED = -1e30
LOG2E = 1.4426950408889634
VMEM_LIMIT = 60 * 2**20
BF = jnp.bfloat16
F32 = jnp.float32
BY_MESH = pl.DeviceIdType.MESH
ANYWHERE = pl.BlockSpec(memory_space=pl.ANY)
IN_VMEM = pl.BlockSpec(memory_space=pltpu.VMEM)
IN_SMEM = pl.BlockSpec(memory_space=pltpu.SMEM)


def nn(left, right):
    return jnp.dot(left, right, preferred_element_type=F32)


def nt(left, right):
    return lax.dot_general(left, right, (((1,), (1,)), ((), ())), preferred_element_type=F32)


def tn(left, right):
    return lax.dot_general(left, right, (((0,), (0,)), ((), ())), preferred_element_type=F32)


def rows_at(start, size):
    return pl.ds(pl.multiple_of(start, 16), size)


def lanes_at(start, size):
    return pl.ds(pl.multiple_of(start, 128), size)


def loop(count, body):
    def step(index, carry):
        body(index)
        return carry

    lax.fori_loop(0, count, step, 0)


class Place:
    def __init__(self):
        dp = lax.axis_index("dp")
        tensor = lax.axis_index("tensor")
        self.dp = dp
        self.z = lax.div(dp, 4)
        self.xl = lax.rem(lax.div(dp, 2), 2)
        self.c = lax.rem(dp, 2)
        self.y = lax.div(tensor, 2)
        self.g = lax.rem(tensor, 2)
        self.x = self.g * 2 + self.xl
        self.sib = self.at(c=1 - self.c)
        self.up = self.at(y=lax.rem(self.y + 1, 4))
        self.down = self.at(y=lax.rem(self.y + 3, 4))
        self.z_up = self.at(z=lax.rem(self.z + 1, 4))
        self.z_down = self.at(z=lax.rem(self.z + 3, 4))
        self.partner = self.at(g=self.c, c=self.g)
        self.home = self.c == self.g
        self.away = self.c != self.g

    def at(self, z=None, x=None, xl=None, c=None, y=None, g=None):
        z = self.z if z is None else z
        c = self.c if c is None else c
        y = self.y if y is None else y
        if x is None:
            xl = self.xl if xl is None else xl
            g = self.g if g is None else g
        else:
            xl = lax.rem(x, 2)
            g = lax.div(x, 2)
        return (z * 4 + xl * 2 + c, y * 2 + g)

    def in_row(self, dx, core):
        return self.at(x=lax.rem(self.x + dx, 4), c=core)

    def row_mates(self):
        return [self.in_row(dx, core) for dx in (1, 2, 3) for core in (0, 1)]

    def column_mates(self):
        return [self.at(z=lax.rem(self.z + dz, 4), c=core) for dz in (1, 2, 3) for core in (0, 1)]

    def ring(self, dy, same):
        return lax.rem(self.y + dy + 4, 4) * 2 + (self.c if same else 1 - self.c)


def greet(devices):
    barrier = pltpu.get_barrier_semaphore()
    for device in devices:
        pl.semaphore_signal(barrier, 1, device_id=device, device_id_type=BY_MESH)
    pl.semaphore_wait(barrier, len(devices))


def remote(src, dst, send, recv, device):
    return pltpu.make_async_remote_copy(
        src_ref=src, dst_ref=dst, send_sem=send, recv_sem=recv, device_id=device, device_id_type=BY_MESH
    )


class Gather:
    SENDS = (
        (0, True, None),
        (0, True, None),
        (0, True, None),
        (-1, True, 0),
        (1, True, 1),
        (-1, True, None),
        (1, True, None),
        (2, True, 0),
        (2, True, 1),
    )
    LANDS = (
        (0, False, None),
        (-1, True, None),
        (1, True, None),
        (2, True, 0),
        (2, True, 1),
        (-1, False, None),
        (1, False, None),
        (2, False, 0),
        (2, False, 1),
    )

    def __init__(self, place, buf, send, recv):
        self.place, self.buf, self.send, self.recv = place, buf, send, recv
        p = place
        self.to = (p.sib, p.up, p.down, p.up, p.down, p.sib, p.sib, p.sib, p.sib)

    def piece(self, what):
        dy, same, half = what
        start = self.place.ring(dy, same) * ROWS
        if half is None:
            return self.buf.at[rows_at(start, ROWS)]
        return self.buf.at[rows_at(start + half * HALF, HALF)]

    def copy(self, i):
        piece = self.piece(self.SENDS[i])
        return remote(piece, piece, self.send.at[i], self.recv.at[i], self.to[i])

    def landed(self, i):
        piece = self.piece(self.LANDS[i])
        remote(piece, piece, self.send.at[i], self.recv.at[i], self.to[i]).wait_recv()

    def begin(self):
        for i in (1, 2, 0):
            self.copy(i).start()

    def near(self):
        self.landed(1)
        self.copy(3).start()
        self.copy(5).start()
        self.landed(2)
        self.copy(4).start()
        self.copy(6).start()

    def far(self):
        self.landed(3)
        self.copy(7).start()
        self.landed(4)
        self.copy(8).start()

    def own_pair(self):
        self.landed(0)

    def near_pairs(self):
        self.landed(5)
        self.landed(6)

    def far_pair(self):
        self.landed(7)
        self.landed(8)

    def end(self):
        for i in range(9):
            self.copy(i).wait_send()


class Scatter:
    def __init__(self, place, part, sib_in, relay, near, send, recv, start=None):
        self.place, self.part, self.sib_in, self.relay, self.near = place, part, sib_in, relay, near
        self.send, self.recv = send, recv
        self.start = start or (lambda dy: place.ring(dy, True) * ROWS)

    def mine(self, dy, half=None):
        start = self.start(dy)
        if half is None:
            return self.part.at[rows_at(start, ROWS)]
        return self.part.at[rows_at(start + half * HALF, HALF)]

    def others(self, dy):
        return self.part.at[rows_at(self.place.ring(dy, False) * ROWS, ROWS)]

    def copy(self, i):
        p = self.place
        if i < 4:
            src, dst, to = self.others(i), self.sib_in.at[i], p.sib
        elif i == 4:
            src, dst, to = self.mine(2, 0), self.relay.at[0], p.up
        elif i == 5:
            src, dst, to = self.mine(2, 1), self.relay.at[1], p.down
        elif i == 6:
            src, dst, to = self.mine(1, 1), self.near.at[0, pl.ds(HALF, HALF)], p.up
        elif i == 7:
            src, dst, to = self.mine(-1, 0), self.near.at[1, pl.ds(0, HALF)], p.down
        elif i == 8:
            src, dst, to = self.mine(1, 0), self.near.at[0, pl.ds(0, HALF)], p.up
        else:
            src, dst, to = self.mine(-1, 1), self.near.at[1, pl.ds(HALF, HALF)], p.down
        return remote(src, dst, self.send.at[i], self.recv.at[i], to)

    def exchange(self, dy):
        self.copy(dy % 4).start()

    def combine(self, dy):
        self.copy(dy % 4).wait_recv()
        add_rows(self.part, self.start(dy), self.sib_in.at[dy % 4], 0, ROWS)

    def relay_out(self):
        self.copy(4).start()
        self.copy(5).start()

    def near_free(self, dy):
        self.copy(6 if dy == 1 else 7).start()

    def near_rest(self):
        self.copy(4).wait_recv()
        add_rows(self.part, self.start(1), self.relay.at[0], 0, HALF)
        self.copy(8).start()
        self.copy(5).wait_recv()
        add_rows(self.part, self.start(-1) + HALF, self.relay.at[1], 0, HALF)
        self.copy(9).start()

    def arrived(self):
        for i in (6, 7, 8, 9):
            self.copy(i).wait_recv()

    def total(self, start, size, lanes):
        own = self.part[rows_at(self.start(0) + start, size), lanes].astype(F32)
        return (
            own
            + self.near[0, rows_at(start, size), lanes].astype(F32)
            + self.near[1, rows_at(start, size), lanes].astype(F32)
        )

    def end(self, first=0):
        for i in range(first, 10):
            self.copy(i).wait_send()


def scatter_scratch():
    return [
        pltpu.VMEM((GROUP, WIDE), BF),
        pltpu.VMEM((4, ROWS, WIDE), BF),
        pltpu.VMEM((2, HALF, WIDE), BF),
        pltpu.VMEM((2, ROWS, WIDE), BF),
        pltpu.SemaphoreType.DMA((10,)),
        pltpu.SemaphoreType.DMA((10,)),
    ]


def gather_scratch():
    return [pltpu.VMEM((GROUP, WIDE), BF), pltpu.SemaphoreType.DMA((9,)), pltpu.SemaphoreType.DMA((9,))]


def add_rows(dst, start, src, src_start, count):
    def body(index):
        at = rows_at(start + index * 16, 16)
        dst[at, :] = (dst[at, :].astype(F32) + src[rows_at(src_start + index * 16, 16), :].astype(F32)).astype(BF)

    loop(count // 16, body)


class Weights:
    def __init__(self, place, piece, full, by_rows, cut, send, recv):
        self.place, self.piece, self.full, self.by_rows = place, piece, full, by_rows
        self.send, self.recv = send, recv
        size = piece.shape[1] if by_rows else piece.shape[0]
        self.parts = (pl.ds(0, cut), pl.ds(cut, size - cut))

    def source(self, half):
        part = self.parts[half]
        return self.piece.at[:, part] if self.by_rows else self.piece.at[part, :]

    def slot(self, index, count, half):
        span = lanes_at(index * 128, count * 128)
        part = self.parts[half]
        return self.full.at[span, part] if self.by_rows else self.full.at[part, span]

    def column(self, dz):
        return lax.rem(self.place.z + dz, 4)

    def first(self):
        p = self.place
        marks = (self.recv.at[p.xl * 2 + p.c], self.recv.at[4 + p.z * 2 + p.c])
        slots = (self.slot(p.dp, 1, 0), self.slot(p.dp, 1, 1))
        for d in (2, 1, 3):
            remote(self.source(0), slots[0], self.send.at[d], marks[0], p.in_row(d, p.g)).start()
            remote(self.source(1), slots[1], self.send.at[4 + d], marks[1], p.at(z=self.column(d), c=p.g)).start()

        @pl.when(p.home)
        def _():
            for half in range(2):
                pltpu.make_async_copy(self.source(half), slots[half], marks[half]).start()

        @pl.when(p.away)
        def _():
            for half in range(2):
                remote(self.source(half), slots[half], self.send.at[4 * half], marks[half], p.sib).start()

    def landed(self, slot, mark):
        remote(slot, slot, self.send.at[0], self.recv.at[mark], self.place.sib).wait_recv()

    def along_z(self, dz):
        block = self.slot(self.place.z * 4, 4, 0)
        return remote(block, block, self.send.at[7 + dz], self.recv.at[11 + dz], self.place.at(z=self.column(dz)))

    def along_x(self, dz, dx):
        p = self.place
        z = self.column(dz)
        pair = self.slot(z * 4 + p.xl * 2, 2, 1)
        return remote(
            pair, pair, self.send.at[10 + dz * 3 + dx], self.recv.at[15 + p.xl * 4 + z], p.in_row(dx, p.c)
        )

    def second(self):
        p = self.place
        for index in range(4):
            self.landed(self.slot(p.z * 4 + index, 1, 0), index)
        for dz in (2, 1, 3):
            self.along_z(dz).start()

        @pl.when(p.home)
        def _():
            for dz in range(4):
                z = self.column(dz)
                for core in range(2):
                    self.landed(self.slot(z * 4 + p.xl * 2 + core, 1, 1), 4 + z * 2 + core)
                for dx in (2, 1, 3):
                    self.along_x(dz, dx).start()

    def arrived(self):
        p = self.place
        for dz in range(1, 4):
            self.landed(self.slot(self.column(4 - dz) * 4, 4, 0), 11 + dz)
        for z in range(4):
            self.landed(self.slot(z * 4 + (1 - p.xl) * 2, 2, 1), 15 + (1 - p.xl) * 4 + z)

        @pl.when(p.away)
        def _():
            for z in range(4):
                self.landed(self.slot(z * 4 + p.xl * 2, 2, 1), 15 + p.xl * 4 + z)

    def end(self):
        p = self.place
        for d in (1, 2, 3):
            for half in range(2):
                slot = self.slot(p.dp, 1, half)
                remote(self.source(half), slot, self.send.at[4 * half + d], self.recv.at[0], p.sib).wait_send()
            self.along_z(d).wait_send()

        @pl.when(p.away)
        def _():
            for half in range(2):
                slot = self.slot(p.dp, 1, half)
                remote(self.source(half), slot, self.send.at[4 * half], self.recv.at[0], p.sib).wait_send()

        @pl.when(p.home)
        def _():
            for dz in range(4):
                for dx in (1, 2, 3):
                    self.along_x(dz, dx).wait_send()


def weight_marks():
    return [pltpu.SemaphoreType.DMA((23,)), pltpu.SemaphoreType.DMA((23,))]


class Swap:
    def __init__(self, place, pairs, send, recv):
        self.place, self.pairs, self.send, self.recv = place, pairs, send, recv

    def begin(self, i):
        src, dst = self.pairs[i]
        p = self.place

        @pl.when(p.home)
        def _():
            pltpu.make_async_copy(src, dst, self.recv.at[i]).start()

        @pl.when(p.away)
        def _():
            remote(src, dst, self.send.at[i], self.recv.at[i], p.partner).start()

    def arrived(self, i):
        src, dst = self.pairs[i]
        remote(src, dst, self.send.at[i], self.recv.at[i], self.place.sib).wait_recv()

    def end(self):
        @pl.when(self.place.away)
        def _():
            for i, (src, dst) in enumerate(self.pairs):
                remote(src, dst, self.send.at[i], self.recv.at[i], self.place.sib).wait_send()


def swap_marks(count):
    return [pltpu.SemaphoreType.DMA((count,)), pltpu.SemaphoreType.DMA((count,))]


def normalise(value):
    mean = jnp.mean(value, axis=-1, keepdims=True)
    center = value - mean
    inverse = lax.rsqrt(jnp.mean(center * center, axis=-1, keepdims=True) + EPS)
    return center * inverse, inverse


def norm_back(value, gain, grad):
    normed, inverse = normalise(value)
    e = grad * gain
    return (e - jnp.mean(e, axis=-1, keepdims=True) - normed * jnp.mean(e * normed, axis=-1, keepdims=True)) * inverse


def pair_rows(place, dy):
    return rows_at(lax.rem(place.y + dy + 4, 4) * PAIR, PAIR)


def wide_product(put, make):
    loop(4, lambda j: put(lanes_at(j * 512, 512), make(lanes_at(j * 512, 512))))
    put(pl.ds(WIDTH, LANES), make(pl.ds(WIDTH, LANES)))


def call(kernel, collective, ins, specs, outs, out_specs, scratch):
    return pl.pallas_call(
        kernel,
        name=kernel.__name__,
        out_shape=outs,
        in_specs=specs,
        out_specs=out_specs,
        scratch_shapes=scratch,
        compiler_params=pltpu.CompilerParams(
            collective_id=collective, has_side_effects=True, vmem_limit_bytes=VMEM_LIMIT
        ),
    )(*ins)


def shape(*dims, kind=BF):
    return jax.ShapeDtypeStruct(dims, kind)


def identity():
    row = lax.broadcasted_iota(jnp.int32, (LANES, LANES), 0)
    return jnp.where(row == lax.broadcasted_iota(jnp.int32, (LANES, LANES), 1), 1.0, 0.0).astype(BF)


def query_info(token_row, start_row):
    token_high = jnp.floor(token_row * (1.0 / 16.0))
    start_high = jnp.floor(start_row * (1.0 / 16.0))
    digit = lax.broadcasted_iota(jnp.int32, (16, GROUP), 0)
    digits = jnp.where(digit == 0, token_high, 0.0)
    digits = jnp.where(digit == 1, token_row - 16.0 * token_high, digits)
    digits = jnp.where(digit == 2, start_high, digits)
    digits = jnp.where(digit == 3, start_row - 16.0 * start_high, digits)
    row = lax.broadcasted_iota(jnp.int32, (16, LANES), 0)
    lane = lax.broadcasted_iota(jnp.int32, (16, LANES), 1)
    worth = jnp.where((row == 0) & (lane == 0) | (row == 2) & (lane == 1), 16.0, 0.0)
    worth = worth + jnp.where((row == 1) & (lane == 0) | (row == 3) & (lane == 1), 1.0, 0.0)
    return tn(digits.astype(BF), worth.astype(BF))


def slope_row(place, head, tokens_row):
    number = (place.ring(0, True) * 2 + head + 1).astype(F32)
    slope = jnp.exp2(jnp.full((1, GROUP), -0.5, F32) * number)
    return slope * LOG2E * tokens_row


def forward_kernel(
    gain, shift, joined_reduce, down_expand, joined_expand, joined_shift, order, output_expand, output_shift,
    second_gain, second_shift, up_reduce, lengths, adapters,
    tokens, cotangent, up_shift, joined_piece, output_piece, output_reduce, up_piece, up_expand, down_piece, down_reduce,
    normed, middle, side_o, context, qkv, mask_own,
    probs_out, side_q, normed_own, gathered_grad, cot_own, joined_full, output_full, up_full, down_full, tokens_own,
    up_shift_own,
    tok_here, aux, aux_here, half_expand, shift_here, joined_here, output_here, info, mask_all, probs,
    rows, rows_send, rows_recv, grads, grads_send, grads_recv, part, sib_in, relay, near, s_send, s_recv,
    w_send, w_recv, o_send, o_recv, u_send, u_recv, d_send, d_recv, swap_send, swap_recv, out_sem, probs_sem,
):
    p = Place()
    greet([p.sib, p.up, p.down] + p.row_mates() + p.column_mates())
    joined = Weights(p, joined_piece, joined_here.at[pl.ds(0, WIDTH)], True, 512, w_send, w_recv)
    output = Weights(p, output_piece, output_here.at[:, pl.ds(0, WIDTH)], False, 128, o_send, o_recv)
    up = Weights(p, up_piece, up_full.at[pl.ds(0, WIDTH)], True, 640, u_send, u_recv)
    down = Weights(p, down_piece, down_full.at[:, pl.ds(0, WIDTH)], False, 512, d_send, d_recv)
    own_rows = rows_at(p.ring(0, True) * ROWS, ROWS)
    their_rows = rows_at((p.y * 2 + p.g) * ROWS, ROWS)
    swap = Swap(
        p,
        [
            (tokens, tok_here),
            (aux, aux_here),
            (half_expand, joined_here.at[pl.ds(WIDTH, LANES)]),
            (joined_shift, shift_here),
            (cotangent, grads.at[their_rows, pl.ds(0, WIDTH)]),
            (output_reduce, output_here.at[:, pl.ds(WIDTH, LANES)]),
            (up_expand, up_full.at[pl.ds(WIDTH, LANES)]),
            (down_reduce, down_full.at[:, pl.ds(WIDTH, LANES)]),
            (up_shift, up_shift_own),
        ],
        swap_send,
        swap_recv,
    )
    swap.begin(0)
    joined.first()
    token = order[...]
    first_end = lengths[0, 0]
    second_end = first_end + lengths[0, 1]
    later = token >= second_end
    late = token >= first_end
    start = jnp.where(later, second_end, jnp.where(late, first_end, 0))
    adapter = jnp.where(later, adapters[0, 2], jnp.where(late, adapters[0, 1], adapters[0, 0]))
    for i, row in enumerate((token, start, adapter)):
        aux[:, pl.ds(i * GROUP, GROUP)] = jnp.broadcast_to(row.astype(F32), (8, GROUP))
    half_expand[...] = (SCALE * joined_expand[...].astype(F32)).astype(BF)
    for i in (1, 2, 3, 4):
        swap.begin(i)
    swap.arrived(1)
    token_row = aux_here[0:1, pl.ds(0, GROUP)]
    info[...] = query_info(token_row, aux_here[0:1, pl.ds(GROUP, GROUP)])
    column = lax.shift_right_logical(lax.broadcasted_iota(jnp.int32, (LANES, GROUP), 0), 4).astype(F32)
    chosen = jnp.where(column == aux_here[0:1, pl.ds(2 * GROUP, GROUP)], 1.0, 0.0).astype(BF)
    mask_all[...] = tn(chosen, identity()).astype(BF)
    mask_own[...] = mask_all[own_rows, :]
    mask_rows = mask_all[own_rows, :].astype(F32)
    joined.second()
    swap.arrived(0)

    def norm_block(index):
        at = rows_at(index * BLOCK, BLOCK)
        value, _ = normalise(tok_here[at, :].astype(F32))
        rows[rows_at(p.ring(0, True) * ROWS + index * BLOCK, BLOCK), pl.ds(0, WIDTH)] = (
            value * gain[...] + shift[...]
        ).astype(BF)

    loop(ROWS // BLOCK, norm_block)
    rows[own_rows, pl.ds(WIDTH, LANES)] = (
        mask_rows * nn(rows[own_rows, pl.ds(0, WIDTH)], joined_reduce[...])
    ).astype(BF)
    gather = Gather(p, rows, rows_send, rows_recv)
    gather_grad = Gather(p, grads, grads_send, grads_recv)
    gather.begin()
    output.first()
    up.first()
    for i in range(5, 9):
        swap.begin(i)
    swap.arrived(4)
    grads[own_rows, pl.ds(WIDTH, LANES)] = (
        mask_rows * (SCALE * nt(grads[own_rows, pl.ds(0, WIDTH)], down_expand[...]))
    ).astype(BF)
    copies = [
        pltpu.make_async_copy(tok_here, tokens_own, out_sem.at[0]),
        pltpu.make_async_copy(grads.at[own_rows, pl.ds(0, WIDTH)], cot_own, out_sem.at[1]),
        pltpu.make_async_copy(rows.at[own_rows, pl.ds(0, WIDTH)], normed_own, out_sem.at[2]),
    ]
    for copy in copies:
        copy.start()
    gather.near()
    gather_grad.begin()
    output.second()
    up.second()
    down.first()
    swap.arrived(2)
    swap.arrived(3)
    joined.arrived()
    copies.append(pltpu.make_async_copy(joined_here, joined_full, out_sem.at[3]))
    copies[-1].start()

    def project(dy):
        at = pair_rows(p, dy)

        def body(j):
            lanes = lanes_at(j * 256, 256)
            qkv[at, lanes] = (nn(rows[at, :], joined_here[:, lanes]) + shift_here[:, lanes]).astype(BF)

        loop(QKV // 256, body)

    gather.own_pair()
    project(0)
    gather.near_pairs()
    project(1)
    project(-1)
    gather.far()
    gather.far_pair()
    project(2)
    copies.append(pltpu.make_async_copy(rows.at[:, pl.ds(WIDTH, LANES)], side_q, out_sem.at[4]))
    copies[-1].start()
    output.arrived()
    swap.arrived(5)
    copies.append(pltpu.make_async_copy(output_here, output_full, out_sem.at[5]))
    copies[-1].start()
    probs_copies = []

    def attend(dy, same):
        at = rows_at(p.ring(dy, same) * ROWS, ROWS)
        n = len(probs_copies)
        if n >= 2:
            probs_copies[n - 2].wait()
        query_token = info[at, 0:1]
        query_start = info[at, 1:2]
        allowed = (token_row <= query_token) & (token_row >= query_start)
        for head in range(2):
            first = head * 3 * HEAD
            scores = nt(qkv[at, first : first + HEAD], qkv[:, first + HEAD : first + 2 * HEAD])
            scores = scores * (LOG2E / math.sqrt(HEAD)) + slope_row(p, head, token_row)
            scores = jnp.where(allowed, scores, MASKED)
            top = jnp.max(scores, axis=-1, keepdims=True)
            weights = jnp.exp2(scores - top)
            total = jnp.sum(weights, axis=-1, keepdims=True)
            weights = (weights * (1.0 / total)).astype(BF)
            probs[n % 2, head] = weights
            context[at, head * HEAD : (head + 1) * HEAD] = nn(
                weights, qkv[:, first + 2 * HEAD : first + 3 * HEAD]
            ).astype(BF)
        copy = pltpu.make_async_copy(probs.at[n % 2], probs_out.at[:, at], probs_sem.at[n])
        copy.start()
        probs_copies.append(copy)

        def put(lanes, value):
            part[at, lanes] = value.astype(BF)

        wide_product(put, lambda lanes: nn(context[at, :], output_here[:, lanes]))

    scatter = Scatter(p, part, sib_in, relay, near, s_send, s_recv)
    attend(2, False)
    scatter.exchange(2)
    attend(2, True)
    scatter.combine(2)
    scatter.relay_out()
    gather_grad.near()
    down.second()
    attend(1, False)
    scatter.exchange(1)
    attend(1, True)
    scatter.combine(1)
    scatter.near_free(1)
    attend(-1, False)
    scatter.exchange(-1)
    attend(-1, True)
    scatter.combine(-1)
    scatter.near_free(-1)
    gather_grad.far()
    attend(0, False)
    scatter.exchange(0)
    scatter.near_rest()
    attend(0, True)
    scatter.combine(0)
    gather_grad.own_pair()
    gather_grad.near_pairs()
    gather_grad.far_pair()
    copies.append(pltpu.make_async_copy(grads, gathered_grad, out_sem.at[6]))
    copies[-1].start()
    scatter.arrived()
    side = (mask_rows * scatter.total(0, ROWS, pl.ds(WIDTH, LANES))).astype(BF)
    side_o[...] = side

    def add_tile(j):
        lanes = lanes_at(j * 512, 512)
        middle[:, lanes] = (
            tok_here[:, lanes].astype(F32)
            + scatter.total(0, ROWS, lanes)
            + output_shift[:, lanes]
            + SCALE * nn(side, output_expand[:, lanes])
        )

    loop(4, add_tile)

    def second_block(index):
        at = rows_at(index * BLOCK, BLOCK)
        value, _ = normalise(middle[at, :])
        normed[at, pl.ds(0, WIDTH)] = (value * second_gain[...] + second_shift[...]).astype(BF)

    loop(ROWS // BLOCK, second_block)
    normed[:, pl.ds(WIDTH, LANES)] = (mask_rows * nn(normed[:, pl.ds(0, WIDTH)], up_reduce[...])).astype(BF)
    up.arrived()
    down.arrived()
    for i in range(6, 9):
        swap.arrived(i)
    swap.end()
    for sender in (gather, gather_grad, scatter, joined, output, up, down):
        sender.end()
    for copy in copies + probs_copies[-2:]:
        copy.wait()


def forward_call(ins):
    outs = [
        shape(ROWS, WIDE), shape(ROWS, WIDTH, kind=F32), shape(ROWS, LANES), shape(GROUP, CTX), shape(GROUP, QKV),
        shape(ROWS, LANES),
        shape(2, GROUP, GROUP), shape(GROUP, LANES), shape(ROWS, WIDTH), shape(GROUP, WIDE), shape(ROWS, WIDTH),
        shape(WIDE, QKV), shape(CTX, WIDE), shape(WIDE, UNITS), shape(UNITS, WIDE), shape(ROWS, WIDTH),
        shape(1, UNITS, kind=F32),
    ]
    return call(
        forward_kernel,
        1,
        ins,
        [IN_VMEM] * 12 + [IN_SMEM] * 2 + [ANYWHERE] * 10,
        outs,
        [IN_VMEM] * 6 + [ANYWHERE] * 11,
        [
            pltpu.VMEM((ROWS, WIDTH), BF), pltpu.VMEM((8, 3 * GROUP), F32), pltpu.VMEM((8, 3 * GROUP), F32),
            pltpu.VMEM((LANES, QKV), BF), pltpu.VMEM((1, QKV), F32), pltpu.VMEM((WIDE, QKV), BF),
            pltpu.VMEM((CTX, WIDE), BF), pltpu.VMEM((GROUP, LANES), F32), pltpu.VMEM((GROUP, LANES), BF),
            pltpu.VMEM((2, 2, ROWS, GROUP), BF), *gather_scratch(), *gather_scratch(), *scatter_scratch(),
            *weight_marks(), *weight_marks(), *weight_marks(), *weight_marks(), *swap_marks(9),
            pltpu.SemaphoreType.DMA((7,)), pltpu.SemaphoreType.DMA((8,)),
        ],
    )


def feed_kernel(
    normed, middle, up_shift, mask, gain, up_reduce, output_expand,
    gathered_grad, up_weights, down_weights,
    grad_out, grad_stage, side_u, by_shard, out_parts,
    up_full, down_full, grads, rows, rows_send, rows_recv, act, slope, part, sib_in, relay, near, s_send, s_recv,
    part_out, sib_in_out, t_send, t_recv, own_sem,
):
    p = Place()
    own_rows = rows_at(p.ring(0, True) * ROWS, ROWS)
    stage = pltpu.make_async_copy(normed, rows.at[own_rows], own_sem.at[0])
    stage.start()
    load_down = pltpu.make_async_copy(down_weights, down_full, own_sem.at[1])
    load_down.start()
    load_grads = pltpu.make_async_copy(gathered_grad, grads, own_sem.at[2])
    load_grads.start()
    load_up = pltpu.make_async_copy(up_weights, up_full, own_sem.at[3])
    load_up.start()
    greet([p.sib, p.up, p.down])
    gather = Gather(p, rows, rows_send, rows_recv)
    stage.wait()
    gather.begin()

    def lift(dy):
        at = pair_rows(p, dy)

        def body(j):
            lanes = lanes_at(j * 256, 256)
            slope[at, lanes] = nt(grads[at, :], down_full[lanes, :]).astype(BF)

        loop(UNITS // 256, body)

    def hide(dy):
        at = pair_rows(p, dy)

        def body(j):
            lanes = lanes_at(j * 256, 256)
            v = nn(rows[at, :], up_full[:, lanes]) + up_shift[:, lanes]
            square = v * v
            t = jnp.tanh(v * (0.7978845608028654 + 0.7978845608028654 * 0.044715 * square))
            half = 0.5 + 0.5 * t
            act[at, lanes] = (v * half).astype(BF)
            bend = half + v * (1.0 - t * t) * (
                0.5 * 0.7978845608028654 + 0.5 * 0.7978845608028654 * 3.0 * 0.044715 * square
            )
            slope[at, lanes] = (slope[at, lanes].astype(F32) * bend).astype(BF)

        loop(UNITS // 256, body)

    def back(dy, same):
        at = rows_at(p.ring(dy, same) * ROWS, ROWS)

        def put(lanes, value):
            part[at, lanes] = value.astype(BF)

        wide_product(put, lambda lanes: nt(slope[at, :], up_full[lanes, :]))

    def forth(dy):
        at = pair_rows(p, dy)

        def put(lanes, value):
            part_out[at, lanes] = value.astype(BF)

        wide_product(put, lambda lanes: nn(act[at, :], down_full[:, lanes]))

    load_down.wait()
    load_grads.wait()
    lift(0)
    lift(1)
    load_up.wait()
    expand = pl.ds(WIDTH, LANES)
    up_full[expand, :] = (SCALE * up_full[expand, :].astype(F32)).astype(BF)
    gather.own_pair()
    hide(0)
    lift(-1)
    gather.near()
    lift(2)
    gather.near_pairs()
    hide(1)
    gather.far()
    hide(-1)
    gather.far_pair()
    hide(2)
    scatter = Scatter(p, part, sib_in, relay, near, s_send, s_recv)
    back(2, False)
    scatter.exchange(2)
    back(2, True)
    scatter.combine(2)
    scatter.relay_out()
    back(1, False)
    scatter.exchange(1)
    back(1, True)
    scatter.combine(1)
    scatter.near_free(1)
    back(-1, False)
    scatter.exchange(-1)
    back(-1, True)
    scatter.combine(-1)
    scatter.near_free(-1)
    back(0, False)
    scatter.exchange(0)
    back(0, True)
    scatter_out = Scatter(p, part_out, sib_in_out, None, None, t_send, t_recv)
    forth(2)
    scatter_out.exchange(2)
    scatter.near_rest()
    scatter.combine(0)
    for dy in (1, -1, 0):
        forth(dy)
        scatter_out.exchange(dy)

    def by_unit(j):
        at = lanes_at(j * 256, 256)
        by_shard[at, :] = tn(act[:, at], grads[:, pl.ds(WIDTH, LANES)]).astype(BF)
        by_shard[lanes_at(UNITS + j * 256, 256), :] = (
            SCALE * tn(slope[:, at], rows[:, pl.ds(WIDTH, LANES)])
        ).astype(BF)

    loop(UNITS // 256, by_unit)
    copies = []
    for dy in (2, 1, -1, 0):
        scatter_out.combine(dy)
        copy = pltpu.make_async_copy(
            scatter_out.mine(dy), out_parts.at[pl.ds(dy % 4 * ROWS, ROWS)], own_sem.at[4 + dy % 4]
        )
        copy.start()
        copies.append(copy)
    scatter.arrived()
    mask_rows = mask[...].astype(F32)
    side_u[...] = (mask_rows * scatter.total(0, ROWS, pl.ds(WIDTH, LANES))).astype(BF)

    def norm_block(index):
        at = rows_at(index * BLOCK, BLOCK)
        mine = rows_at(p.ring(0, True) * ROWS + index * BLOCK, BLOCK)
        grad = scatter.total(index * BLOCK, BLOCK, pl.ds(0, WIDTH)) + nt(side_u[at, :], up_reduce[...])
        grad = grads[mine, pl.ds(0, WIDTH)].astype(F32) + norm_back(middle[at, :], gain[...], grad)
        grad_out[at, :] = grad
        grad_stage[at, pl.ds(0, WIDTH)] = grad.astype(BF)

    loop(ROWS // BLOCK, norm_block)
    grad_stage[:, pl.ds(WIDTH, LANES)] = (
        mask_rows * (SCALE * nt(grad_stage[:, pl.ds(0, WIDTH)], output_expand[...]))
    ).astype(BF)
    gather.end()
    scatter.end()
    for dy in range(4):
        scatter_out.copy(dy).wait_send()
    for copy in copies:
        copy.wait()


def feed_call(ins):
    outs = [
        shape(ROWS, WIDTH, kind=F32), shape(ROWS, WIDE), shape(ROWS, LANES), shape(2 * UNITS, LANES),
        shape(4 * ROWS, WIDE),
    ]
    scratch = scatter_scratch()
    return call(
        feed_kernel,
        2,
        ins,
        [IN_VMEM] * 7 + [ANYWHERE] * 3,
        outs,
        [IN_VMEM] * 4 + [ANYWHERE],
        [
            pltpu.VMEM((WIDE, UNITS), BF), pltpu.VMEM((UNITS, WIDE), BF), pltpu.VMEM((GROUP, WIDE), BF),
            *gather_scratch(), pltpu.VMEM((GROUP, UNITS), BF), pltpu.VMEM((GROUP, UNITS), BF), *scratch,
            scratch[0], scratch[1], scratch[4], scratch[5], pltpu.SemaphoreType.DMA((8,)),
        ],
    )


class Reducer:
    def __init__(self, place, by_shard, whole, refs):
        self.p, self.by_shard, self.whole = place, by_shard, whole
        (
            self.shard_in, self.shard_sum, self.shard_all, self.sib_in, self.here, self.slices_in, self.slice_sum,
            self.bits_in, self.bit_sum, self.whole_all,
            self.a_send, self.a_recv, self.b_send, self.b_recv, self.c_send, self.c_recv, self.d_send, self.d_recv,
            self.e_send, self.e_recv, self.f_send, self.f_recv, self.g_send, self.g_recv, self.mark,
        ) = refs
        self.m = place.z * 4 + place.x
        self.cut = by_shard.shape[0] // 16
        self.half = whole.shape[0] // 2
        self.slice = self.half // 16
        self.bit = self.slice // 4
        self.sent = []

    @staticmethod
    def scratch(shard_rows, whole_rows):
        dma = pltpu.SemaphoreType.DMA
        cut, half = shard_rows // 16, whole_rows // 2
        piece = half // 16
        return [
            pltpu.VMEM((16, cut, LANES), BF), pltpu.VMEM((cut, LANES), BF), pltpu.VMEM((shard_rows, LANES), BF),
            pltpu.VMEM((half, LANES), BF), pltpu.VMEM((half, LANES), BF), pltpu.VMEM((16, piece, LANES), BF),
            pltpu.VMEM((piece, LANES), BF), pltpu.VMEM((4, piece // 4, LANES), BF), pltpu.VMEM((piece // 4, LANES), BF),
            pltpu.VMEM((whole_rows, LANES), BF),
            dma((16,)), dma((16,)), dma((16,)), dma((16,)), dma((16,)), dma((16,)), dma((4,)), dma((4,)),
            dma((4,)), dma((4,)), dma((2,)), dma((2,)), dma((16,)), dma((16,)), dma((1,)),
        ]

    @staticmethod
    def mates(place):
        m = place.z * 4 + place.x
        mates = []
        for k in range(1, 16):
            other = lax.rem(m + k, 16)
            for core in (0, 1):
                mates.append(place.at(z=lax.div(other, 4), x=lax.rem(other, 4), c=core))
        return mates + [place.at(y=lax.rem(place.y + 2, 4))]

    def member(self, k):
        other = lax.rem(self.m + k, 16)
        return other, self.p.at(z=lax.div(other, 4), x=lax.rem(other, 4))

    def push(self, src, dst, send, recv, device):
        copy = remote(src, dst, send, recv, device)
        copy.start()
        self.sent.append(copy)
        return copy

    def await_at(self, dst, recv):
        remote(dst, dst, self.f_send.at[0], recv, self.p.sib).wait_recv()

    def open(self):
        there = rows_at((1 - self.p.c) * self.half, self.half)
        self.push(self.whole.at[there], self.sib_in, self.f_send.at[0], self.f_recv.at[0], self.p.sib)
        self.open_shard()

    def open_shard(self):
        for k in range(1, 16):
            other, device = self.member(k)
            piece = self.by_shard.at[rows_at(other * self.cut, self.cut)]
            self.push(piece, self.shard_in.at[k], self.a_send.at[k], self.a_recv.at[k], device)

    def halves(self):
        self.await_at(self.sib_in, self.f_recv.at[0])

        def body(index):
            at = rows_at(index * 128, 128)
            mine = self.whole[rows_at(self.p.c * self.half + index * 128, 128), :].astype(F32)
            self.here[at, :] = (mine + self.sib_in[at, :].astype(F32)).astype(BF)

        loop(self.half // 128, body)
        for k in range(1, 16):
            other, device = self.member(k)
            piece = self.here.at[rows_at(other * self.slice, self.slice)]
            self.push(piece, self.slices_in.at[k], self.b_send.at[k], self.b_recv.at[k], device)

    def shards(self):
        p = self.p
        total = self.by_shard[rows_at(self.m * self.cut, self.cut), :].astype(F32)
        for k in range(1, 16):
            self.await_at(self.shard_in.at[k], self.a_recv.at[k])
            total = total + self.shard_in[k].astype(F32)
        self.shard_sum[...] = total.astype(BF)
        mine = self.shard_all.at[rows_at(self.m * self.cut, self.cut)]
        mark = self.c_recv.at[self.m]
        for n in range(1, 16):
            device = p.at(
                z=lax.rem(p.z + n // 4, 4), xl=lax.rem(p.xl + n // 2 % 2, 2), g=p.c, c=lax.rem(p.c + n % 2, 2)
            )
            self.push(self.shard_sum, mine, self.c_send.at[n], mark, device)
        self.swapped = remote(self.shard_sum, mine, self.c_send.at[0], mark, p.at(g=p.c))
        pl.when(p.away)(self.swapped.start)
        pl.when(p.home)(pltpu.make_async_copy(self.shard_sum, mine, mark).start)

    def slices(self):
        total = self.here[rows_at(self.m * self.slice, self.slice), :].astype(F32)
        for k in range(1, 16):
            self.await_at(self.slices_in.at[k], self.b_recv.at[k])
            total = total + self.slices_in[k].astype(F32)
        self.slice_sum[...] = total.astype(BF)
        for dy in (2, 1, 3):
            other = lax.rem(self.p.y + dy, 4)
            piece = self.slice_sum.at[rows_at(other * self.bit, self.bit)]
            self.push(piece, self.bits_in.at[dy], self.d_send.at[dy], self.d_recv.at[dy], self.p.at(y=other))

    def bits(self):
        total = self.slice_sum[rows_at(self.p.y * self.bit, self.bit), :].astype(F32)
        for dy in (1, 3, 2):
            self.await_at(self.bits_in.at[dy], self.d_recv.at[dy])
            total = total + self.bits_in[dy].astype(F32)
        self.bit_sum[...] = total.astype(BF)
        self.base = self.p.c * self.half + self.m * self.slice
        own = self.whole_all.at[rows_at(self.base + self.p.y * self.bit, self.bit)]
        self.placed = pltpu.make_async_copy(self.bit_sum, own, self.mark.at[0])
        self.placed.start()
        for dy in (2, 1, 3):
            device = self.p.at(y=lax.rem(self.p.y + dy, 4))
            self.push(self.bit_sum, own, self.e_send.at[dy], self.e_recv.at[dy], device)

    def slices_back(self):
        self.placed.wait()
        for dy in (1, 3, 2):
            source = lax.rem(self.p.y + 4 - dy, 4)
            self.await_at(self.whole_all.at[rows_at(self.base + source * self.bit, self.bit)], self.e_recv.at[dy])
        own = self.whole_all.at[rows_at(self.base, self.slice)]
        for k in range(1, 16):
            self.push(own, own, self.g_send.at[k], self.g_recv.at[k], self.member(k)[1])

    def halves_back(self):
        for k in range(1, 16):
            source = lax.rem(self.m + 16 - k, 16)
            landing = self.whole_all.at[rows_at(self.p.c * self.half + source * self.slice, self.slice)]
            self.await_at(landing, self.g_recv.at[k])
        half = self.whole_all.at[rows_at(self.p.c * self.half, self.half)]
        self.push(half, half, self.f_send.at[1], self.f_recv.at[1], self.p.sib)

    def close(self):
        for index in range(16):
            self.await_at(self.shard_all.at[pl.ds(index * self.cut, self.cut)], self.c_recv.at[index])
        self.await_at(self.whole_all.at[rows_at((1 - self.p.c) * self.half, self.half)], self.f_recv.at[1])
        for copy in self.sent:
            copy.wait_send()
        pl.when(self.p.away)(self.swapped.wait_send)


def back_kernel(
    grad_stage, output_full, qkv, tokens, gain, mask, cotangent, down_shift, down_expand, joined_reduce, normed, side_q,
    grad, middle, context, second_normed, side_u, side_o, shard_early,
    joined_weights, out_parts, probs_in,
    block_out, input_grad, by_shard, whole, shard_done, whole_done,
    rows, rows_send, rows_recv, probs, key_grad, value_grad, joined_grad, result, block_own, joined_full, whole_early,
    part, sib_in, relay, near, s_send, s_recv, parts, relay_out, near_out, t_send, t_recv, swap_send, swap_recv, own_sem,
    *reduce_refs,
):
    p = Place()
    own_rows = rows_at(p.ring(0, True) * ROWS, ROWS)
    stage = pltpu.make_async_copy(grad_stage, rows.at[own_rows], own_sem.at[0])
    stage.start()
    loads = []
    for dy in (0, 1, -1, 2):
        at = pair_rows(p, dy)
        load = pltpu.make_async_copy(probs_in.at[:, at], probs.at[:, at], own_sem.at[1 + dy % 4])
        load.start()
        loads.append(load)
    load_parts = pltpu.make_async_copy(out_parts, parts, own_sem.at[5])
    load_parts.start()
    load_joined = pltpu.make_async_copy(joined_weights, joined_full, own_sem.at[6])
    load_joined.start()
    greet([p.sib, p.up, p.down] + Reducer.mates(p))
    gather = Gather(p, rows, rows_send, rows_recv)
    stage.wait()
    gather.begin()
    swap = Swap(p, [(block_own, block_out), (result, input_grad)], swap_send, swap_recv)
    reducer = Reducer(p, shard_early, whole_early, reduce_refs)

    def early_column(j):
        lanes = lanes_at(j * 256, 256)
        whole_early[lanes, :] = tn(second_normed[:, lanes], side_u[...]).astype(BF)
        whole_early[lanes_at(WIDTH + j * 256, 256), :] = (SCALE * tn(grad_stage[:, lanes], side_o[...])).astype(BF)

    loop(WIDTH // 256, early_column)
    reducer.open()

    def back(dy):
        base = lax.rem(p.y + dy + 4, 4) * PAIR

        def body(index):
            at = rows_at(base + index * ROWS, ROWS)
            context_grad = nt(rows[at, :], output_full[...]).astype(BF)
            for head in range(2):
                start = head * 3 * HEAD
                query = qkv[at, start : start + HEAD]
                key = qkv[:, start + HEAD : start + 2 * HEAD]
                value = qkv[:, start + 2 * HEAD : start + 3 * HEAD]
                own = context_grad[:, head * HEAD : (head + 1) * HEAD]
                weights = probs[head, at, :]
                mean = jnp.sum(
                    own.astype(F32) * context[at, head * HEAD : (head + 1) * HEAD].astype(F32), axis=-1, keepdims=True
                )
                score_grad = weights * (nt(own, value) - mean).astype(BF)
                joined_grad[at, start : start + HEAD] = (nn(score_grad, key) * (1.0 / math.sqrt(HEAD))).astype(BF)
                value_grad[head] = value_grad[head] + tn(own, weights)
                key_grad[head] = key_grad[head] + tn(query, score_grad)

        loop(2, body)

    value_grad[...] = jnp.zeros_like(value_grad)
    key_grad[...] = jnp.zeros_like(key_grad)
    scatter_out = Scatter(p, parts, None, relay_out, near_out, t_send, t_recv, lambda dy: dy % 4 * ROWS)
    gather.own_pair()
    loads[0].wait()
    back(0)
    reducer.halves()
    gather.near()
    load_parts.wait()
    scatter_out.relay_out()
    scatter_out.near_free(1)
    scatter_out.near_free(-1)
    gather.near_pairs()
    loads[1].wait()
    back(1)
    gather.far()
    reducer.shards()
    loads[2].wait()
    back(-1)
    reducer.slices()
    gather.far_pair()
    loads[3].wait()
    back(2)
    reducer.bits()
    scatter_out.near_rest()
    turn = identity()
    for head in range(2):
        start = head * 3 * HEAD
        joined_grad[:, start + HEAD : start + 2 * HEAD] = tn(
            (key_grad[head] * (1.0 / math.sqrt(HEAD))).astype(BF), turn
        ).astype(BF)
        joined_grad[:, start + 2 * HEAD : start + 3 * HEAD] = tn(value_grad[head].astype(BF), turn).astype(BF)
    load_joined.wait()

    def product(dy, same):
        at = rows_at(p.ring(dy, same) * ROWS, ROWS)

        def put(lanes, value):
            part[at, lanes] = value.astype(BF)

        wide_product(put, lambda lanes: nt(joined_grad[at, :], joined_full[lanes, :]))

    scatter = Scatter(p, part, sib_in, relay, near, s_send, s_recv)
    product(2, False)
    scatter.exchange(2)
    product(2, True)
    scatter.combine(2)
    scatter.relay_out()
    product(1, False)
    scatter.exchange(1)
    product(1, True)
    scatter.combine(1)
    scatter.near_free(1)
    product(-1, False)
    scatter.exchange(-1)
    product(-1, True)
    scatter.combine(-1)
    scatter.near_free(-1)
    product(0, False)
    scatter.exchange(0)
    product(0, True)
    reducer.slices_back()
    scatter.near_rest()
    scatter.combine(0)
    by_shard[pl.ds(0, CTX), :] = tn(context[...], rows[:, pl.ds(WIDTH, LANES)]).astype(BF)

    def by_lane(j):
        lanes = lanes_at(j * 256, 256)
        by_shard[lanes_at(CTX + j * 256, 256), :] = (SCALE * tn(joined_grad[:, lanes], side_q[...])).astype(BF)

    loop(QKV // 256, by_lane)
    scatter_out.arrived()
    mask_rows = mask[...].astype(F32)
    side_d = (mask_rows * scatter_out.total(0, ROWS, pl.ds(WIDTH, LANES))).astype(BF)

    def add_tile(j):
        lanes = lanes_at(j * 256, 256)
        block_own[:, lanes] = (
            middle[:, lanes]
            + scatter_out.total(0, ROWS, lanes)
            + down_shift[:, lanes]
            + SCALE * nn(side_d, down_expand[:, lanes])
        ).astype(BF)
        whole[lanes, :] = (SCALE * tn(cotangent[:, lanes], side_d)).astype(BF)

    loop(WIDTH // 256, add_tile)
    swap.begin(0)
    reducer.halves_back()
    scatter.arrived()
    side = (mask_rows * scatter.total(0, ROWS, pl.ds(WIDTH, LANES))).astype(BF)

    def norm_block(index):
        at = rows_at(index * BLOCK, BLOCK)
        side_rows = (mask[at, :].astype(F32) * scatter.total(index * BLOCK, BLOCK, pl.ds(WIDTH, LANES))).astype(BF)
        back_grad = scatter.total(index * BLOCK, BLOCK, pl.ds(0, WIDTH)) + nt(side_rows, joined_reduce[...])
        result[at, :] = (grad[at, :] + norm_back(tokens[at, :].astype(F32), gain[...], back_grad)).astype(BF)

    loop(ROWS // BLOCK, norm_block)
    swap.begin(1)

    def by_column(j):
        lanes = lanes_at(j * 256, 256)
        whole[lanes_at(WIDTH + j * 256, 256), :] = tn(normed[:, lanes], side).astype(BF)

    loop(WIDTH // 256, by_column)
    reducer.close()
    shard_done[...] = reducer.shard_all[...]
    whole_done[...] = reducer.whole_all[...]
    gather.end()
    scatter.end()
    scatter_out.end(4)
    swap.arrived(0)
    swap.arrived(1)
    swap.end()


def back_call(ins):
    outs = [
        shape(ROWS, WIDTH), shape(ROWS, WIDTH), shape(CTX + QKV, LANES), shape(2 * WIDTH, LANES),
        shape(2 * UNITS, LANES), shape(2 * WIDTH, LANES),
    ]
    scratch = scatter_scratch()
    return call(
        back_kernel,
        3,
        ins,
        [IN_VMEM] * 19 + [ANYWHERE] * 3,
        outs,
        [ANYWHERE] * 2 + [IN_VMEM] * 4,
        [
            *gather_scratch(), pltpu.VMEM((2, GROUP, GROUP), BF), pltpu.VMEM((2, HEAD, GROUP), F32),
            pltpu.VMEM((2, HEAD, GROUP), F32), pltpu.VMEM((GROUP, QKV), BF), pltpu.VMEM((ROWS, WIDTH), BF),
            pltpu.VMEM((ROWS, WIDTH), BF), pltpu.VMEM((WIDE, QKV), BF), pltpu.VMEM((2 * WIDTH, LANES), BF), *scratch,
            pltpu.VMEM((4 * ROWS, WIDE), BF), *scratch[2:], *swap_marks(2), pltpu.SemaphoreType.DMA((7,)),
            *Reducer.scratch(2 * UNITS, 2 * WIDTH),
        ],
    )


def reduce_kernel(by_shard, whole, shard_out, whole_out, *refs):
    p = Place()
    greet([p.sib, p.up, p.down] + Reducer.mates(p))
    reducer = Reducer(p, by_shard, whole, refs)
    reducer.open()
    reducer.halves()
    reducer.shards()
    reducer.slices()
    reducer.bits()
    reducer.slices_back()
    reducer.halves_back()
    reducer.close()
    shard_out[...] = reducer.shard_all[...]
    whole_out[...] = reducer.whole_all[...]


def reduce_call(ins):
    return call(
        reduce_kernel,
        4,
        ins,
        [IN_VMEM] * 2,
        [shape(CTX + QKV, LANES), shape(2 * WIDTH, LANES)],
        [IN_VMEM] * 2,
        Reducer.scratch(CTX + QKV, 2 * WIDTH),
    )


def finish_kernel(
    shard_early, whole_early, shard_late, whole_late, block_in, grad_in,
    block_out, input_grad, qkv_a, qkv_b, out_a, out_b, up_a, up_b, down_a, down_b,
):
    turn = identity()

    def turned(source, start, out, count):
        def body(j):
            out[0, :, lanes_at(j * 256, 256)] = nt(turn, source[lanes_at(start + j * 256, 256), :])

        loop(count // 256, body)

    def widened(source, out):
        def body(index):
            at = rows_at(index * BLOCK, BLOCK)
            out[at, :] = source[at, :].astype(F32)

        loop(ROWS // BLOCK, body)

    widened(block_in, block_out)
    widened(grad_in, input_grad)
    down_a[0] = shard_early[pl.ds(0, UNITS), :].astype(F32)
    turned(shard_early, UNITS, up_b, UNITS)
    out_a[0] = shard_late[pl.ds(0, CTX), :].astype(F32)
    turned(shard_late, CTX, qkv_b, QKV)
    up_a[0] = whole_early[pl.ds(0, WIDTH), :].astype(F32)
    turned(whole_early, WIDTH, out_b, WIDTH)
    turned(whole_late, 0, down_b, WIDTH)
    qkv_a[0] = whole_late[pl.ds(WIDTH, WIDTH), :].astype(F32)


def finish_call(ins):
    return pl.pallas_call(
        finish_kernel,
        name="finish_kernel",
        out_shape=[
            shape(ROWS, WIDTH, kind=F32), shape(ROWS, WIDTH, kind=F32), shape(1, WIDTH, LANES, kind=F32),
            shape(1, LANES, QKV, kind=F32), shape(1, CTX, LANES, kind=F32), shape(1, LANES, WIDTH, kind=F32),
            shape(1, WIDTH, LANES, kind=F32), shape(1, LANES, UNITS, kind=F32), shape(1, UNITS, LANES, kind=F32),
            shape(1, LANES, WIDTH, kind=F32),
        ],
        in_specs=[IN_VMEM] * 6,
        out_specs=[IN_VMEM] * 10,
        compiler_params=pltpu.CompilerParams(vmem_limit_bytes=VMEM_LIMIT),
    )(*ins)


def shards(
    tokens, lengths, order, sequence_adapter, first_norm_gain, first_norm_bias, second_norm_gain, second_norm_bias,
    joined_matrix, joined_offset_bias, output_matrix, output_offset_bias, up_matrix, up_offset_bias, down_matrix,
    down_offset_bias, joined_adapter_reduce, joined_adapter_expand, output_adapter_reduce, output_adapter_expand,
    up_adapter_reduce, up_adapter_expand, down_adapter_reduce, down_adapter_expand, cotangent,
):
    (
        normed, middle, side_o, context, qkv, mask_own, probs, side_q, normed_first, gathered_grad, cot_own,
        joined_full, output_full, up_full, down_full, tokens_own, up_shift_own,
    ) = forward_call(
        (
            first_norm_gain, first_norm_bias, joined_adapter_reduce[0], down_adapter_expand[0],
            joined_adapter_expand[0], joined_offset_bias, order, output_adapter_expand[0], output_offset_bias,
            second_norm_gain, second_norm_bias, up_adapter_reduce[0], lengths, sequence_adapter,
            tokens, cotangent, up_offset_bias, joined_matrix[0], output_matrix[0], output_adapter_reduce[0],
            up_matrix[0], up_adapter_expand[0], down_matrix[0], down_adapter_reduce[0],
        )
    )
    grad, grad_stage, side_u, shard_feed, out_parts = feed_call(
        (
            normed, middle, up_shift_own, mask_own, second_norm_gain, up_adapter_reduce[0],
            output_adapter_expand[0], gathered_grad, up_full, down_full,
        )
    )
    block_own, input_own, shard_back, whole_back, shard_early, whole_early = back_call(
        (
            grad_stage, output_full, qkv, tokens_own, first_norm_gain, mask_own, cot_own, down_offset_bias,
            down_adapter_expand[0], joined_adapter_reduce[0], normed_first, side_q, grad, middle, context,
            normed, side_u, side_o, shard_feed, joined_full, out_parts, probs,
        )
    )
    shard_late, whole_late = reduce_call((shard_back, whole_back))
    return tuple(finish_call((shard_early, whole_early, shard_late, whole_late, block_own, input_own)))


def solution(mesh):
    spread = P(("dp", "tensor"), None)
    by_dp = P("dp", None)
    rows = P(None, "dp", "tensor")
    cols = P(None, "tensor", "dp")
    last = P(None, None, "tensor")
    middle = P(None, "tensor", None)
    vector = P(None, "tensor")
    return jax.shard_map(
        shards,
        mesh=mesh,
        in_specs=(
            spread, by_dp, by_dp, by_dp, P(), P(), P(), P(), rows, vector, cols, P(), rows, vector, cols, P(),
            P(), last, middle, P(), P(), last, middle, P(), spread,
        ),
        out_specs=(spread, spread, P(), last, middle, P(), P(), last, middle, P()),
        check_vma=False,
    )
```

profile of v0, /device:TPU:1, one launch (start us, length us, event | category | flops | bytes accessed | tf_op | source)
XLA Modules:
  0.0 352.9 jit_solution(14106499147191943959)
XLA Ops:
  0.7 127.7 %forward_kernel.1 = (bf16[160,2176]{1,0:T(8,128)(2,1)}, f32[160,2048]{1,0:T(8,128)}, bf16[160,128]{1,0:T(8,128)(2,1)}, bf16[1280,256]{1,0:T(8,128)(2,1)}, bf16[1...) custom-call(f32[1,2048]{1,0:T(1,128)} %gain.5, ...), custom_call_target="tpu_custom_call" | custom-call | tf_op jit(solution)/shard_map/forward_kernel/pallas_call | solution.py:454
  128.3 72.2 %feed_kernel.1 = (f32[160,2048]{1,0:T(8,128)}, bf16[160,2176]{1,0:T(8,128)(2,1)}, bf16[160,128]{1,0:T(8,128)(2,1)}, bf16[2048,128]{1,0:T(8,128)(2,1)}, bf16[640,2176]{1,0:T(8,128)(2,1)}) custom-call(bf16[160,2176]{1,0:T(8,128)(2,1)} %get-tuple-element.40.normed.second_normed, f32[160,2048]{1,0:T(8,128)} %get-tuple-element.41.middle, ...), custom_call_target="tpu_custom_call" | custom-call | tf_op jit(solution)/shard_map/feed_kernel/pallas_call | solution.py:454
  200.6 105.4 %back_kernel.1 = (bf16[160,2048]{1,0:T(8,128)(2,1)}, bf16[160,2048]{1,0:T(8,128)(2,1)}, bf16[1024,128]{1,0:T(8,128)(2,1)}, bf16[4096,128]{1,0:T(8,128)(2,1)}, bf...) custom-call(bf16[160,2176]{1,0:T(8,128)(2,1)} %get-tuple-element.47.grad_stage, ...), custom_call_target="tpu_custom_call" | custom-call | tf_op jit(solution)/shard_map/back_kernel/pallas_call | solution.py:454
  305.9 37.1 %reduce_kernel.1 = (bf16[1024,128]{1,0:T(8,128)(2,1)}, bf16[4096,128]{1,0:T(8,128)(2,1)}) custom-call(bf16[1024,128]{1,0:T(8,128)(2,1)} %get-tuple-element.64.by_shard, bf16[4096,128]{1,0:T(8,128)(2,1)} %get-tuple-element.65.whole), custom_call_target="tpu_custom_call" | custom-call | tf_op jit(solution)/shard_map/reduce_kernel/pallas_call | solution.py:454
  343.0 9.5 %finish_kernel.1 = (f32[160,2048]{1,0:T(8,128)}, f32[160,2048]{1,0:T(8,128)}, f32[1,2048,128]{2,1,0:T(8,128)}, f32[1,128,768]{2,1,0:T(8,128)}, f32[1,256,128]{2,...) custom-call(bf16[2048,128]{1,0:T(8,128)(2,1)} %get-tuple-element.62., ...), custom_call_target="tpu_custom_call" | custom-call | tf_op jit(solution)/shard_map/finish_kernel/pallas_call | solution.py:1318
where the time goes:
time: 359 us; the launch traced here: 353 us
  Pallas kernels  352 us (98%)
    pallas_call x4, Pallas kernels, call(): pl.pallas_call(kernel, name=kernel.__name__, out_shape=outs, in_specs=spe...  342 us
    pallas_call x1, Pallas kernels, finish_call(): pl.pallas_call(finish_kernel, name='finish_kernel', out_shape=[shape(ROWS...  9.48 us

commit v1 on v0

--- a/solution.py
+++ b/solution.py
@@ -102,6 +102,13 @@
     def column_mates(self):
         return [self.at(z=lax.rem(self.z + dz, 4), c=core) for dz in (1, 2, 3) for core in (0, 1)]
 
+    def ring_mates(self):
+        mates = [self.sib]
+        for dy in (1, 2, 3):
+            y = lax.rem(self.y + dy, 4)
+            mates += [self.at(y=y), self.at(y=y, c=1 - self.c)]
+        return mates
+
     def ring(self, dy, same):
         return lax.rem(self.y + dy + 4, 4) * 2 + (self.c if same else 1 - self.c)
 
@@ -264,17 +271,17 @@
             + self.near[1, rows_at(start, size), lanes].astype(F32)
         )
 
-    def end(self, first=0):
-        for i in range(first, 10):
+    def end(self, first=0, last=10):
+        for i in range(first, last):
             self.copy(i).wait_send()
 
 
-def scatter_scratch():
+def scatter_scratch(width=WIDE):
     return [
-        pltpu.VMEM((GROUP, WIDE), BF),
-        pltpu.VMEM((4, ROWS, WIDE), BF),
-        pltpu.VMEM((2, HALF, WIDE), BF),
-        pltpu.VMEM((2, ROWS, WIDE), BF),
+        pltpu.VMEM((GROUP, width), BF),
+        pltpu.VMEM((4, ROWS, width), BF),
+        pltpu.VMEM((2, HALF, width), BF),
+        pltpu.VMEM((2, ROWS, width), BF),
         pltpu.SemaphoreType.DMA((10,)),
         pltpu.SemaphoreType.DMA((10,)),
     ]
@@ -332,45 +339,67 @@
     def landed(self, slot, mark):
         remote(slot, slot, self.send.at[0], self.recv.at[mark], self.place.sib).wait_recv()
 
-    def along_z(self, dz):
-        block = self.slot(self.place.z * 4, 4, 0)
-        return remote(block, block, self.send.at[7 + dz], self.recv.at[11 + dz], self.place.at(z=self.column(dz)))
-
-    def along_x(self, dz, dx):
+    def along_z(self, i):
         p = self.place
-        z = self.column(dz)
+        z, first, count, to = (
+            (p.z, 0, 4, p.z_up),
+            (p.z, 0, 4, p.z_down),
+            (self.column(3), 0, 2, p.z_up),
+            (self.column(1), 2, 2, p.z_down),
+        )[i]
+        block = self.slot(z * 4 + first, count, 0)
+        return remote(block, block, self.send.at[8 + i], self.recv.at[12 + i], to)
+
+    def along_x(self, z, dx):
+        p = self.place
         pair = self.slot(z * 4 + p.xl * 2, 2, 1)
-        return remote(
-            pair, pair, self.send.at[10 + dz * 3 + dx], self.recv.at[15 + p.xl * 4 + z], p.in_row(dx, p.c)
-        )
+        mark = self.send.at[12 + z * 2 + dx // 2]
+        return remote(pair, pair, mark, self.recv.at[16 + p.xl * 4 + z], p.in_row(dx, p.c))
 
     def second(self):
         p = self.place
         for index in range(4):
             self.landed(self.slot(p.z * 4 + index, 1, 0), index)
-        for dz in (2, 1, 3):
-            self.along_z(dz).start()
+        self.along_z(0).start()
+        self.along_z(1).start()
 
         @pl.when(p.home)
         def _():
-            for dz in range(4):
-                z = self.column(dz)
+            for z in range(4):
                 for core in range(2):
                     self.landed(self.slot(z * 4 + p.xl * 2 + core, 1, 1), 4 + z * 2 + core)
-                for dx in (2, 1, 3):
-                    self.along_x(dz, dx).start()
+                self.along_x(z, 1).start()
+                self.along_x(z, 3).start()
+
+    def passed_on(self, i):
+        p = self.place
+        home = 1 - lax.rem(p.c + p.g, 2)
+        plus = 1 - lax.rem(p.xl + home, 2)
+        z = (1 - plus) * 2 + i
+        pair = self.slot(z * 4 + (1 - p.xl) * 2, 2, 1)
+        mark = self.recv.at[16 + (1 - p.xl) * 4 + z]
+        return remote(pair, pair, self.send.at[20 + i], mark, p.in_row(3 - 2 * plus, p.c))
+
+    def third(self):
+        p = self.place
+        self.landed(self.slot(self.column(3) * 4, 4, 0), 12)
+        self.along_z(2).start()
+        self.landed(self.slot(self.column(1) * 4, 4, 0), 13)
+        self.along_z(3).start()
+        for z in range(4):
+            self.landed(self.slot(z * 4 + (1 - p.xl) * 2, 2, 1), 16 + (1 - p.xl) * 4 + z)
+        for i in range(2):
+            self.passed_on(i).start()
 
     def arrived(self):
         p = self.place
-        for dz in range(1, 4):
-            self.landed(self.slot(self.column(4 - dz) * 4, 4, 0), 11 + dz)
-        for z in range(4):
-            self.landed(self.slot(z * 4 + (1 - p.xl) * 2, 2, 1), 15 + (1 - p.xl) * 4 + z)
+        self.landed(self.slot(self.column(2) * 4, 2, 0), 14)
+        self.landed(self.slot(self.column(2) * 4 + 2, 2, 0), 15)
 
         @pl.when(p.away)
         def _():
             for z in range(4):
-                self.landed(self.slot(z * 4 + p.xl * 2, 2, 1), 15 + p.xl * 4 + z)
+                self.landed(self.slot(z * 4 + p.xl * 2, 2, 1), 16 + p.xl * 4 + z)
 
     def end(self):
         p = self.place
@@ -378,7 +407,10 @@
             for half in range(2):
                 slot = self.slot(p.dp, 1, half)
                 remote(self.source(half), slot, self.send.at[4 * half + d], self.recv.at[0], p.sib).wait_send()
-            self.along_z(d).wait_send()
+        for i in range(4):
+            self.along_z(i).wait_send()
+        for i in range(2):
+            self.passed_on(i).wait_send()
 
         @pl.when(p.away)
         def _():
@@ -388,13 +420,13 @@
 
         @pl.when(p.home)
         def _():
-            for dz in range(4):
-                for dx in (1, 2, 3):
-                    self.along_x(dz, dx).wait_send()
+            for z in range(4):
+                self.along_x(z, 1).wait_send()
+                self.along_x(z, 3).wait_send()
 
 
 def weight_marks():
-    return [pltpu.SemaphoreType.DMA((23,)), pltpu.SemaphoreType.DMA((23,))]
+    return [pltpu.SemaphoreType.DMA((22,)), pltpu.SemaphoreType.DMA((24,))]
 
 
 class Swap:
@@ -508,9 +540,9 @@
     p = Place()
     greet([p.sib, p.up, p.down] + p.row_mates() + p.column_mates())
     joined = Weights(p, joined_piece, joined_here.at[pl.ds(0, WIDTH)], True, 512, w_send, w_recv)
-    output = Weights(p, output_piece, output_here.at[:, pl.ds(0, WIDTH)], False, 128, o_send, o_recv)
+    output = Weights(p, output_piece, output_here.at[:, pl.ds(0, WIDTH)], False, 160, o_send, o_recv)
     up = Weights(p, up_piece, up_full.at[pl.ds(0, WIDTH)], True, 640, u_send, u_recv)
-    down = Weights(p, down_piece, down_full.at[:, pl.ds(0, WIDTH)], False, 512, d_send, d_recv)
+    down = Weights(p, down_piece, down_full.at[:, pl.ds(0, WIDTH)], False, 640, d_send, d_recv)
     own_rows = rows_at(p.ring(0, True) * ROWS, ROWS)
     their_rows = rows_at((p.y * 2 + p.g) * ROWS, ROWS)
     swap = Swap(
@@ -529,8 +561,8 @@
         swap_send,
         swap_recv,
     )
+    joined.first()
     swap.begin(0)
-    joined.first()
     token = order[...]
     first_end = lengths[0, 0]
     second_end = first_end + lengths[0, 1]
@@ -541,7 +573,7 @@
     for i, row in enumerate((token, start, adapter)):
         aux[:, pl.ds(i * GROUP, GROUP)] = jnp.broadcast_to(row.astype(F32), (8, GROUP))
     half_expand[...] = (SCALE * joined_expand[...].astype(F32)).astype(BF)
-    for i in (1, 2, 3, 4):
+    for i in (1, 2, 3):
         swap.begin(i)
     swap.arrived(1)
     token_row = aux_here[0:1, pl.ds(0, GROUP)]
@@ -568,10 +600,14 @@
     gather = Gather(p, rows, rows_send, rows_recv)
     gather_grad = Gather(p, grads, grads_send, grads_recv)
     gather.begin()
+    swap.begin(4)
     output.first()
+    joined.third()
     up.first()
+    down.first()
     for i in range(5, 9):
         swap.begin(i)
+    output.second()
     swap.arrived(4)
     grads[own_rows, pl.ds(WIDTH, LANES)] = (
         mask_rows * (SCALE * nt(grads[own_rows, pl.ds(0, WIDTH)], down_expand[...]))
@@ -585,9 +621,7 @@
         copy.start()
     gather.near()
     gather_grad.begin()
-    output.second()
     up.second()
-    down.first()
     swap.arrived(2)
     swap.arrived(3)
     joined.arrived()
@@ -607,10 +641,13 @@
     project(0)
     gather.near_pairs()
     project(1)
+    output.third()
     project(-1)
     gather.far()
+    down.second()
     gather.far_pair()
     project(2)
+    up.third()
     copies.append(pltpu.make_async_copy(rows.at[:, pl.ds(WIDTH, LANES)], side_q, out_sem.at[4]))
     copies[-1].start()
     output.arrived()
@@ -656,12 +693,12 @@
     scatter.combine(2)
     scatter.relay_out()
     gather_grad.near()
-    down.second()
     attend(1, False)
     scatter.exchange(1)
     attend(1, True)
     scatter.combine(1)
     scatter.near_free(1)
+    down.third()
     attend(-1, False)
     scatter.exchange(-1)
     attend(-1, True)
@@ -759,14 +796,9 @@
     stage.wait()
     gather.begin()
 
-    def lift(dy):
-        at = pair_rows(p, dy)
-
-        def body(j):
-            lanes = lanes_at(j * 256, 256)
-            slope[at, lanes] = nt(grads[at, :], down_full[lanes, :]).astype(BF)
-
-        loop(UNITS // 256, body)
+    def lift(j):
+        lanes = lanes_at(j * 256, 256)
+        slope[:, lanes] = nt(grads[...], down_full[lanes, :]).astype(BF)
 
     def hide(dy):
         at = pair_rows(p, dy)
@@ -785,8 +817,8 @@
 
         loop(UNITS // 256, body)
 
-    def back(dy, same):
-        at = rows_at(p.ring(dy, same) * ROWS, ROWS)
+    def back(dy):
+        at = pair_rows(p, dy)
 
         def put(lanes, value):
             part[at, lanes] = value.astype(BF)
@@ -803,42 +835,35 @@
 
     load_down.wait()
     load_grads.wait()
-    lift(0)
-    lift(1)
+    loop(UNITS // 256, lift)
     load_up.wait()
     expand = pl.ds(WIDTH, LANES)
     up_full[expand, :] = (SCALE * up_full[expand, :].astype(F32)).astype(BF)
+    scatter = Scatter(p, part, sib_in, relay, near, s_send, s_recv)
+    scatter_out = Scatter(p, part_out, sib_in_out, None, None, t_send, t_recv)
     gather.own_pair()
     hide(0)
-    lift(-1)
     gather.near()
-    lift(2)
     gather.near_pairs()
     hide(1)
+    hide(-1)
     gather.far()
-    hide(-1)
     gather.far_pair()
     hide(2)
-    scatter = Scatter(p, part, sib_in, relay, near, s_send, s_recv)
-    back(2, False)
+    back(2)
     scatter.exchange(2)
-    back(2, True)
+    back(1)
+    scatter.exchange(1)
     scatter.combine(2)
     scatter.relay_out()
-    back(1, False)
-    scatter.exchange(1)
-    back(1, True)
+    back(-1)
+    scatter.exchange(-1)
     scatter.combine(1)
     scatter.near_free(1)
-    back(-1, False)
-    scatter.exchange(-1)
-    back(-1, True)
     scatter.combine(-1)
     scatter.near_free(-1)
-    back(0, False)
+    back(0)
     scatter.exchange(0)
-    back(0, True)
-    scatter_out = Scatter(p, part_out, sib_in_out, None, None, t_send, t_recv)
     forth(2)
     scatter_out.exchange(2)
     scatter.near_rest()
@@ -855,14 +880,17 @@
         ).astype(BF)
 
     loop(UNITS // 256, by_unit)
+    for dy in range(4):
+        scatter_out.combine(dy)
     copies = []
-    for dy in (2, 1, -1, 0):
-        scatter_out.combine(dy)
-        copy = pltpu.make_async_copy(
-            scatter_out.mine(dy), out_parts.at[pl.ds(dy % 4 * ROWS, ROWS)], own_sem.at[4 + dy % 4]
-        )
+
+    def hand_on(src, start, count):
+        copy = pltpu.make_async_copy(src, out_parts.at[pl.ds(start, count)], own_sem.at[4 + len(copies)])
         copy.start()
         copies.append(copy)
+
+    for dy in range(4):
+        hand_on(scatter_out.mine(dy), dy * ROWS, ROWS)
     scatter.arrived()
     mask_rows = mask[...].astype(F32)
     side_u[...] = (mask_rows * scatter.total(0, ROWS, pl.ds(WIDTH, LANES))).astype(BF)
@@ -881,8 +909,7 @@
     ).astype(BF)
     gather.end()
     scatter.end()
-    for dy in range(4):
-        scatter_out.copy(dy).wait_send()
+    scatter_out.end(0, 4)
     for copy in copies:
         copy.wait()
 
@@ -909,34 +936,10 @@
 
 
 class Reducer:
-    def __init__(self, place, by_shard, whole, refs):
-        self.p, self.by_shard, self.whole = place, by_shard, whole
-        (
-            self.shard_in, self.shard_sum, self.shard_all, self.sib_in, self.here, self.slices_in, self.slice_sum,
-            self.bits_in, self.bit_sum, self.whole_all,
-            self.a_send, self.a_recv, self.b_send, self.b_recv, self.c_send, self.c_recv, self.d_send, self.d_recv,
-            self.e_send, self.e_recv, self.f_send, self.f_recv, self.g_send, self.g_recv, self.mark,
-        ) = refs
+    def __init__(self, place, source, sib_mark):
+        self.p, self.source, self.sib_mark = place, source, sib_mark
         self.m = place.z * 4 + place.x
-        self.cut = by_shard.shape[0] // 16
-        self.half = whole.shape[0] // 2
-        self.slice = self.half // 16
-        self.bit = self.slice // 4
         self.sent = []
-
-    @staticmethod
-    def scratch(shard_rows, whole_rows):
-        dma = pltpu.SemaphoreType.DMA
-        cut, half = shard_rows // 16, whole_rows // 2
-        piece = half // 16
-        return [
-            pltpu.VMEM((16, cut, LANES), BF), pltpu.VMEM((cut, LANES), BF), pltpu.VMEM((shard_rows, LANES), BF),
-            pltpu.VMEM((half, LANES), BF), pltpu.VMEM((half, LANES), BF), pltpu.VMEM((16, piece, LANES), BF),
-            pltpu.VMEM((piece, LANES), BF), pltpu.VMEM((4, piece // 4, LANES), BF), pltpu.VMEM((piece // 4, LANES), BF),
-            pltpu.VMEM((whole_rows, LANES), BF),
-            dma((16,)), dma((16,)), dma((16,)), dma((16,)), dma((16,)), dma((16,)), dma((4,)), dma((4,)),
-            dma((4,)), dma((4,)), dma((2,)), dma((2,)), dma((16,)), dma((16,)), dma((1,)),
-        ]
 
     @staticmethod
     def mates(place):
@@ -946,7 +949,7 @@
             other = lax.rem(m + k, 16)
             for core in (0, 1):
                 mates.append(place.at(z=lax.div(other, 4), x=lax.rem(other, 4), c=core))
-        return mates + [place.at(y=lax.rem(place.y + 2, 4))]
+        return mates
 
     def member(self, k):
         other = lax.rem(self.m + k, 16)
@@ -956,59 +959,112 @@
         copy = remote(src, dst, send, recv, device)
         copy.start()
         self.sent.append(copy)
-        return copy
 
     def await_at(self, dst, recv):
-        remote(dst, dst, self.f_send.at[0], recv, self.p.sib).wait_recv()
+        remote(dst, dst, self.sib_mark, recv, self.p.sib).wait_recv()
+
+    def close(self):
+        for copy in self.sent:
+            copy.wait_send()
+
+
+class ShardSum(Reducer):
+    def __init__(self, place, source, refs):
+        (
+            self.landing, self.total, self.all, self.a_send, self.a_recv, self.c_send, self.c_recv,
+        ) = refs
+        super().__init__(place, source, self.a_send.at[0])
+        self.cut = source.shape[0] // 16
+
+    @staticmethod
+    def scratch(count):
+        dma = pltpu.SemaphoreType.DMA
+        cut = count // 16
+        return [
+            pltpu.VMEM((16, cut, LANES), BF), pltpu.VMEM((cut, LANES), BF), pltpu.VMEM((count, LANES), BF),
+            dma((16,)), dma((16,)), dma((16,)), dma((16,)),
+        ]
 
     def open(self):
-        there = rows_at((1 - self.p.c) * self.half, self.half)
-        self.push(self.whole.at[there], self.sib_in, self.f_send.at[0], self.f_recv.at[0], self.p.sib)
-        self.open_shard()
-
-    def open_shard(self):
         for k in range(1, 16):
             other, device = self.member(k)
-            piece = self.by_shard.at[rows_at(other * self.cut, self.cut)]
-            self.push(piece, self.shard_in.at[k], self.a_send.at[k], self.a_recv.at[k], device)
-
-    def halves(self):
-        self.await_at(self.sib_in, self.f_recv.at[0])
-
-        def body(index):
-            at = rows_at(index * 128, 128)
-            mine = self.whole[rows_at(self.p.c * self.half + index * 128, 128), :].astype(F32)
-            self.here[at, :] = (mine + self.sib_in[at, :].astype(F32)).astype(BF)
-
-        loop(self.half // 128, body)
+            piece = self.source.at[rows_at(other * self.cut, self.cut)]
+            self.push(piece, self.landing.at[k], self.a_send.at[k], self.a_recv.at[k], device)
+
+    def spread(self):
+        p = self.p
+        total = self.source[rows_at(self.m * self.cut, self.cut), :].astype(F32)
         for k in range(1, 16):
-            other, device = self.member(k)
-            piece = self.here.at[rows_at(other * self.slice, self.slice)]
-            self.push(piece, self.slices_in.at[k], self.b_send.at[k], self.b_recv.at[k], device)
-
-    def shards(self):
-        p = self.p
-        total = self.by_shard[rows_at(self.m * self.cut, self.cut), :].astype(F32)
-        for k in range(1, 16):
-            self.await_at(self.shard_in.at[k], self.a_recv.at[k])
-            total = total + self.shard_in[k].astype(F32)
-        self.shard_sum[...] = total.astype(BF)
-        mine = self.shard_all.at[rows_at(self.m * self.cut, self.cut)]
+            self.await_at(self.landing.at[k], self.a_recv.at[k])
+            total = total + self.landing[k].astype(F32)
+        self.total[...] = total.astype(BF)
+        mine = self.all.at[rows_at(self.m * self.cut, self.cut)]
         mark = self.c_recv.at[self.m]
         for n in range(1, 16):
             device = p.at(
                 z=lax.rem(p.z + n // 4, 4), xl=lax.rem(p.xl + n // 2 % 2, 2), g=p.c, c=lax.rem(p.c + n % 2, 2)
             )
-            self.push(self.shard_sum, mine, self.c_send.at[n], mark, device)
-        self.swapped = remote(self.shard_sum, mine, self.c_send.at[0], mark, p.at(g=p.c))
+            self.push(self.total, mine, self.c_send.at[n], mark, device)
+        self.swapped = remote(self.total, mine, self.c_send.at[0], mark, p.at(g=p.c))
         pl.when(p.away)(self.swapped.start)
-        pl.when(p.home)(pltpu.make_async_copy(self.shard_sum, mine, mark).start)
+        pl.when(p.home)(pltpu.make_async_copy(self.total, mine, mark).start)
+
+    def close(self):
+        for index in range(16):
+            self.await_at(self.all.at[pl.ds(index * self.cut, self.cut)], self.c_recv.at[index])
+        super().close()
+        pl.when(self.p.away)(self.swapped.wait_send)
+
+
+class WholeSum(Reducer):
+    def __init__(self, place, source, refs):
+        (
+            self.sib_in, self.here, self.landing, self.slice_sum, self.bits_in, self.bit_sum, self.all,
+            self.b_send, self.b_recv, self.d_send, self.d_recv, self.e_send, self.e_recv, self.f_send, self.f_recv,
+            self.g_send, self.g_recv, self.mark,
+        ) = refs
+        super().__init__(place, source, self.f_send.at[0])
+        self.half = source.shape[0] // 2
+        self.slice = self.half // 16
+        self.bit = self.slice // 4
+        self.base = place.c * self.half + self.m * self.slice
+
+    @staticmethod
+    def scratch(count):
+        dma = pltpu.SemaphoreType.DMA
+        half = count // 2
+        piece = half // 16
+        return [
+            pltpu.VMEM((half, LANES), BF), pltpu.VMEM((half, LANES), BF), pltpu.VMEM((16, piece, LANES), BF),
+            pltpu.VMEM((piece, LANES), BF), pltpu.VMEM((4, piece // 4, LANES), BF), pltpu.VMEM((piece // 4, LANES), BF),
+            pltpu.VMEM((count, LANES), BF),
+            dma((16,)), dma((16,)), dma((4,)), dma((4,)), dma((4,)), dma((4,)), dma((2,)), dma((2,)),
+            dma((16,)), dma((16,)), dma((1,)),
+        ]
+
+    def open(self):
+        there = rows_at((1 - self.p.c) * self.half, self.half)
+        self.push(self.source.at[there], self.sib_in, self.f_send.at[0], self.f_recv.at[0], self.p.sib)
+
+    def halves(self):
+        self.await_at(self.sib_in, self.f_recv.at[0])
+
+        def body(index):
+            at = rows_at(index * 128, 128)
+            mine = self.source[rows_at(self.p.c * self.half + index * 128, 128), :].astype(F32)
+            self.here[at, :] = (mine + self.sib_in[at, :].astype(F32)).astype(BF)
+
+        loop(self.half // 128, body)
+        for k in range(1, 16):
+            other, device = self.member(k)
+            piece = self.here.at[rows_at(other * self.slice, self.slice)]
+            self.push(piece, self.landing.at[k], self.b_send.at[k], self.b_recv.at[k], device)
 
     def slices(self):
         total = self.here[rows_at(self.m * self.slice, self.slice), :].astype(F32)
         for k in range(1, 16):
-            self.await_at(self.slices_in.at[k], self.b_recv.at[k])
-            total = total + self.slices_in[k].astype(F32)
+            self.await_at(self.landing.at[k], self.b_recv.at[k])
+            total = total + self.landing[k].astype(F32)
         self.slice_sum[...] = total.astype(BF)
         for dy in (2, 1, 3):
             other = lax.rem(self.p.y + dy, 4)
@@ -1021,8 +1077,7 @@
             self.await_at(self.bits_in.at[dy], self.d_recv.at[dy])
             total = total + self.bits_in[dy].astype(F32)
         self.bit_sum[...] = total.astype(BF)
-        self.base = self.p.c * self.half + self.m * self.slice
-        own = self.whole_all.at[rows_at(self.base + self.p.y * self.bit, self.bit)]
+        own = self.all.at[rows_at(self.base + self.p.y * self.bit, self.bit)]
         self.placed = pltpu.make_async_copy(self.bit_sum, own, self.mark.at[0])
         self.placed.start()
         for dy in (2, 1, 3):
@@ -1033,57 +1088,59 @@
         self.placed.wait()
         for dy in (1, 3, 2):
             source = lax.rem(self.p.y + 4 - dy, 4)
-            self.await_at(self.whole_all.at[rows_at(self.base + source * self.bit, self.bit)], self.e_recv.at[dy])
-        own = self.whole_all.at[rows_at(self.base, self.slice)]
+            self.await_at(self.all.at[rows_at(self.base + source * self.bit, self.bit)], self.e_recv.at[dy])
+        own = self.all.at[rows_at(self.base, self.slice)]
         for k in range(1, 16):
             self.push(own, own, self.g_send.at[k], self.g_recv.at[k], self.member(k)[1])
 
     def halves_back(self):
         for k in range(1, 16):
             source = lax.rem(self.m + 16 - k, 16)
-            landing = self.whole_all.at[rows_at(self.p.c * self.half + source * self.slice, self.slice)]
+            landing = self.all.at[rows_at(self.p.c * self.half + source * self.slice, self.slice)]
             self.await_at(landing, self.g_recv.at[k])
-        half = self.whole_all.at[rows_at(self.p.c * self.half, self.half)]
+        half = self.all.at[rows_at(self.p.c * self.half, self.half)]
         self.push(half, half, self.f_send.at[1], self.f_recv.at[1], self.p.sib)
 
     def close(self):
-        for index in range(16):
-            self.await_at(self.shard_all.at[pl.ds(index * self.cut, self.cut)], self.c_recv.at[index])
-        self.await_at(self.whole_all.at[rows_at((1 - self.p.c) * self.half, self.half)], self.f_recv.at[1])
-        for copy in self.sent:
-            copy.wait_send()
-        pl.when(self.p.away)(self.swapped.wait_send)
+        self.await_at(self.all.at[rows_at((1 - self.p.c) * self.half, self.half)], self.f_recv.at[1])
+        super().close()
 
 
 def back_kernel(
     grad_stage, output_full, qkv, tokens, gain, mask, cotangent, down_shift, down_expand, joined_reduce, normed, side_q,
     grad, middle, context, second_normed, side_u, side_o, shard_early,
     joined_weights, out_parts, probs_in,
-    block_out, input_grad, by_shard, whole, shard_done, whole_done,
+    block_out, input_grad, shard_done, shard_rest, whole_done, whole_rest,
     rows, rows_send, rows_recv, probs, key_grad, value_grad, joined_grad, result, block_own, joined_full, whole_early,
+    shard_late, whole_late, side_part, side_in, side_send, side_recv,
     part, sib_in, relay, near, s_send, s_recv, parts, relay_out, near_out, t_send, t_recv, swap_send, swap_recv, own_sem,
-    *reduce_refs,
+    *refs,
 ):
     p = Place()
     own_rows = rows_at(p.ring(0, True) * ROWS, ROWS)
-    stage = pltpu.make_async_copy(grad_stage, rows.at[own_rows], own_sem.at[0])
-    stage.start()
     loads = []
+
+    def load(src, dst):
+        copy = pltpu.make_async_copy(src, dst, own_sem.at[len(loads)])
+        copy.start()
+        loads.append(copy)
+
+    load(grad_stage, rows.at[own_rows])
     for dy in (0, 1, -1, 2):
         at = pair_rows(p, dy)
-        load = pltpu.make_async_copy(probs_in.at[:, at], probs.at[:, at], own_sem.at[1 + dy % 4])
-        load.start()
-        loads.append(load)
-    load_parts = pltpu.make_async_copy(out_parts, parts, own_sem.at[5])
-    load_parts.start()
-    load_joined = pltpu.make_async_copy(joined_weights, joined_full, own_sem.at[6])
-    load_joined.start()
-    greet([p.sib, p.up, p.down] + Reducer.mates(p))
+        load(probs_in.at[:, at], probs.at[:, at])
+    load(out_parts, parts)
+    load(joined_weights, joined_full)
+    greet(p.ring_mates() + Reducer.mates(p))
     gather = Gather(p, rows, rows_send, rows_recv)
-    stage.wait()
+    loads[0].wait()
     gather.begin()
     swap = Swap(p, [(block_own, block_out), (result, input_grad)], swap_send, swap_recv)
-    reducer = Reducer(p, shard_early, whole_early, reduce_refs)
+    early_shard = ShardSum(p, shard_early, refs[0:7])
+    early_whole = WholeSum(p, whole_early, refs[7:25])
+    late_shard = ShardSum(p, shard_late, refs[25:32])
+    late_whole = WholeSum(p, whole_late, refs[32:50])
+    early_shard.open()
 
     def early_column(j):
         lanes = lanes_at(j * 256, 256)
@@ -1091,7 +1148,7 @@
         whole_early[lanes_at(WIDTH + j * 256, 256), :] = (SCALE * tn(grad_stage[:, lanes], side_o[...])).astype(BF)
 
     loop(WIDTH // 256, early_column)
-    reducer.open()
+    early_whole.open()
 
     def back(dy):
         base = lax.rem(p.y + dy + 4, 4) * PAIR
@@ -1120,27 +1177,27 @@
     key_grad[...] = jnp.zeros_like(key_grad)
     scatter_out = Scatter(p, parts, None, relay_out, near_out, t_send, t_recv, lambda dy: dy % 4 * ROWS)
     gather.own_pair()
-    loads[0].wait()
+    loads[1].wait()
     back(0)
-    reducer.halves()
+    early_whole.halves()
+    loads[5].wait()
     gather.near()
-    load_parts.wait()
     scatter_out.relay_out()
     scatter_out.near_free(1)
     scatter_out.near_free(-1)
     gather.near_pairs()
-    loads[1].wait()
+    loads[2].wait()
     back(1)
     gather.far()
-    reducer.shards()
-    loads[2].wait()
+    early_shard.spread()
+    loads[3].wait()
     back(-1)
-    reducer.slices()
+    early_whole.slices()
     gather.far_pair()
-    loads[3].wait()
+    scatter_out.near_rest()
+    loads[4].wait()
     back(2)
-    reducer.bits()
-    scatter_out.near_rest()
+    early_whole.bits()
     turn = identity()
     for head in range(2):
         start = head * 3 * HEAD
@@ -1148,48 +1205,71 @@
             (key_grad[head] * (1.0 / math.sqrt(HEAD))).astype(BF), turn
         ).astype(BF)
         joined_grad[:, start + 2 * HEAD : start + 3 * HEAD] = tn(value_grad[head].astype(BF), turn).astype(BF)
-    load_joined.wait()
-
-    def product(dy, same):
-        at = rows_at(p.ring(dy, same) * ROWS, ROWS)
-
-        def put(lanes, value):
-            part[at, lanes] = value.astype(BF)
-
-        wide_product(put, lambda lanes: nt(joined_grad[at, :], joined_full[lanes, :]))
+    loads[6].wait()
+
+    def product(dy):
+        at = pair_rows(p, dy)
+
+        def body(j):
+            lanes = lanes_at(j * 512, 512)
+            part[at, lanes] = nt(joined_grad[at, :], joined_full[lanes, :]).astype(BF)
+
+        loop(WIDTH // 512, body)
 
     scatter = Scatter(p, part, sib_in, relay, near, s_send, s_recv)
-    product(2, False)
+    product(2)
     scatter.exchange(2)
-    product(2, True)
+    side_part[...] = nt(joined_grad[...], joined_full[pl.ds(WIDTH, LANES), :]).astype(BF)
+    side_copies = []
+    for k in range(1, 8):
+        dy, same = k // 2, k % 2 == 0
+        y, core = lax.rem(p.y + dy, 4), (p.c if same else 1 - p.c)
+        copy = remote(
+            side_part.at[rows_at((y * 2 + core) * ROWS, ROWS)], side_in.at[k], side_send.at[k], side_recv.at[k],
+            p.at(y=y, c=core),
+        )
+        copy.start()
+        side_copies.append(copy)
     scatter.combine(2)
     scatter.relay_out()
-    product(1, False)
+    product(1)
     scatter.exchange(1)
-    product(1, True)
+    product(-1)
+    scatter.exchange(-1)
     scatter.combine(1)
     scatter.near_free(1)
-    product(-1, False)
-    scatter.exchange(-1)
-    product(-1, True)
     scatter.combine(-1)
     scatter.near_free(-1)
-    product(0, False)
+    mask_rows = mask[...].astype(F32)
+    side_total = side_part[own_rows, :].astype(F32)
+    for k in range(1, 8):
+        side_copies[k - 1].wait_recv()
+        side_total = side_total + side_in[k].astype(F32)
+    side_part[own_rows, :] = (mask_rows * side_total).astype(BF)
+    scatter_out.arrived()
+    side_d = (mask_rows * scatter_out.total(0, ROWS, pl.ds(WIDTH, LANES))).astype(BF)
+
+    def late_column(j):
+        lanes = lanes_at(j * 256, 256)
+        whole_late[lanes, :] = (SCALE * tn(cotangent[:, lanes], side_d)).astype(BF)
+        whole_late[lanes_at(WIDTH + j * 256, 256), :] = tn(normed[:, lanes], side_part[own_rows, :]).astype(BF)
+
+    loop(WIDTH // 256, late_column)
+    late_whole.open()
+    product(0)
     scatter.exchange(0)
-    product(0, True)
-    reducer.slices_back()
     scatter.near_rest()
+    late_whole.halves()
     scatter.combine(0)
-    by_shard[pl.ds(0, CTX), :] = tn(context[...], rows[:, pl.ds(WIDTH, LANES)]).astype(BF)
-
-    def by_lane(j):
+    shard_late[pl.ds(0, CTX), :] = tn(context[...], rows[:, pl.ds(WIDTH, LANES)]).astype(BF)
+
+    def late_lane(j):
         lanes = lanes_at(j * 256, 256)
-        by_shard[lanes_at(CTX + j * 256, 256), :] = (SCALE * tn(joined_grad[:, lanes], side_q[...])).astype(BF)
-
-    loop(QKV // 256, by_lane)
-    scatter_out.arrived()
-    mask_rows = mask[...].astype(F32)
-    side_d = (mask_rows * scatter_out.total(0, ROWS, pl.ds(WIDTH, LANES))).astype(BF)
+        shard_late[lanes_at(CTX + j * 256, 256), :] = (SCALE * tn(joined_grad[:, lanes], side_q[...])).astype(BF)
+
+    loop(QKV // 256, late_lane)
+    late_shard.open()
+    early_whole.slices_back()
 
     def add_tile(j):
         lanes = lanes_at(j * 256, 256)
@@ -1199,34 +1279,38 @@
             + down_shift[:, lanes]
             + SCALE * nn(side_d, down_expand[:, lanes])
         ).astype(BF)
-        whole[lanes, :] = (SCALE * tn(cotangent[:, lanes], side_d)).astype(BF)
 
     loop(WIDTH // 256, add_tile)
     swap.begin(0)
-    reducer.halves_back()
+    late_whole.slices()
+    late_shard.spread()
+    late_whole.bits()
+    late_whole.slices_back()
     scatter.arrived()
-    side = (mask_rows * scatter.total(0, ROWS, pl.ds(WIDTH, LANES))).astype(BF)
 
     def norm_block(index):
         at = rows_at(index * BLOCK, BLOCK)
-        side_rows = (mask[at, :].astype(F32) * scatter.total(index * BLOCK, BLOCK, pl.ds(WIDTH, LANES))).astype(BF)
-        back_grad = scatter.total(index * BLOCK, BLOCK, pl.ds(0, WIDTH)) + nt(side_rows, joined_reduce[...])
+        side = side_part[rows_at(p.ring(0, True) * ROWS + index * BLOCK, BLOCK), :]
+        back_grad = scatter.total(index * BLOCK, BLOCK, pl.ds(0, WIDTH)) + nt(side, joined_reduce[...])
         result[at, :] = (grad[at, :] + norm_back(tokens[at, :].astype(F32), gain[...], back_grad)).astype(BF)
 
     loop(ROWS // BLOCK, norm_block)
     swap.begin(1)
-
-    def by_column(j):
-        lanes = lanes_at(j * 256, 256)
-        whole[lanes_at(WIDTH + j * 256, 256), :] = tn(normed[:, lanes], side).astype(BF)
-
-    loop(WIDTH // 256, by_column)
-    reducer.close()
-    shard_done[...] = reducer.shard_all[...]
-    whole_done[...] = reducer.whole_all[...]
+    early_whole.halves_back()
+    late_whole.halves_back()
+    early_shard.close()
+    late_shard.close()
+    early_whole.close()
+    late_whole.close()
+    shard_done[...] = early_shard.all[...]
+    shard_rest[...] = late_shard.all[...]
+    whole_done[...] = early_whole.all[...]
+    whole_rest[...] = late_whole.all[...]
     gather.end()
     scatter.end()
     scatter_out.end(4)
+    for copy in side_copies:
+        copy.wait_send()
     swap.arrived(0)
     swap.arrived(1)
     swap.end()
@@ -1234,9 +1318,10 @@
 
 def back_call(ins):
     outs = [
-        shape(ROWS, WIDTH), shape(ROWS, WIDTH), shape(CTX + QKV, LANES), shape(2 * WIDTH, LANES),
-        shape(2 * UNITS, LANES), shape(2 * WIDTH, LANES),
+        shape(ROWS, WIDTH), shape(ROWS, WIDTH), shape(2 * UNITS, LANES), shape(CTX + QKV, LANES),
+        shape(2 * WIDTH, LANES), shape(2 * WIDTH, LANES),
     ]
+    dma = pltpu.SemaphoreType.DMA
     scratch = scatter_scratch()
     return call(
         back_kernel,
@@ -1248,70 +1333,67 @@
         [
             *gather_scratch(), pltpu.VMEM((2, GROUP, GROUP), BF), pltpu.VMEM((2, HEAD, GROUP), F32),
             pltpu.VMEM((2, HEAD, GROUP), F32), pltpu.VMEM((GROUP, QKV), BF), pltpu.VMEM((ROWS, WIDTH), BF),
-            pltpu.VMEM((ROWS, WIDTH), BF), pltpu.VMEM((WIDE, QKV), BF), pltpu.VMEM((2 * WIDTH, LANES), BF), *scratch,
-            pltpu.VMEM((4 * ROWS, WIDE), BF), *scratch[2:], *swap_marks(2), pltpu.SemaphoreType.DMA((7,)),
-            *Reducer.scratch(2 * UNITS, 2 * WIDTH),
+            pltpu.VMEM((ROWS, WIDTH), BF), pltpu.VMEM((WIDE, QKV), BF), pltpu.VMEM((2 * WIDTH, LANES), BF),
+            pltpu.VMEM((CTX + QKV, LANES), BF), pltpu.VMEM((2 * WIDTH, LANES), BF), pltpu.VMEM((GROUP, LANES), BF),
+            pltpu.VMEM((8, ROWS, LANES), BF), dma((8,)), dma((8,)), *scatter_scratch(WIDTH),
+            pltpu.VMEM((4 * ROWS, WIDE), BF), *scratch[2:], *swap_marks(2), dma((7,)),
+            *ShardSum.scratch(2 * UNITS), *WholeSum.scratch(2 * WIDTH), *ShardSum.scratch(CTX + QKV),
+            *WholeSum.scratch(2 * WIDTH),
         ],
-    )
-
-
-def reduce_kernel(by_shard, whole, shard_out, whole_out, *refs):
-    p = Place()
-    greet([p.sib, p.up, p.down] + Reducer.mates(p))
-    reducer = Reducer(p, by_shard, whole, refs)
-    reducer.open()
-    reducer.halves()
-    reducer.shards()
-    reducer.slices()
-    reducer.bits()
-    reducer.slices_back()
-    reducer.halves_back()
-    reducer.close()
-    shard_out[...] = reducer.shard_all[...]
-    whole_out[...] = reducer.whole_all[...]
-
-
-def reduce_call(ins):
-    return call(
-        reduce_kernel,
-        4,
-        ins,
-        [IN_VMEM] * 2,
-        [shape(CTX + QKV, LANES), shape(2 * WIDTH, LANES)],
-        [IN_VMEM] * 2,
-        Reducer.scratch(CTX + QKV, 2 * WIDTH),
     )
 
 
 def finish_kernel(
     shard_early, whole_early, shard_late, whole_late, block_in, grad_in,
     block_out, input_grad, qkv_a, qkv_b, out_a, out_b, up_a, up_b, down_a, down_b,
+    block_here, grad_here, a_here, b_here, out_sem,
 ):
     turn = identity()
-
-    def turned(source, start, out, count):
+    copies = []
+
+    def send(src, dst):
+        copy = pltpu.make_async_copy(src, dst, out_sem.at[len(copies)])
+        copy.start()
+        copies.append(copy)
+
+    def turned(source, start, base, count):
         def body(j):
-            out[0, :, lanes_at(j * 256, 256)] = nt(turn, source[lanes_at(start + j * 256, 256), :])
+            b_here[:, lanes_at(base + j * 256, 256)] = nt(turn, source[lanes_at(start + j * 256, 256), :])
 
         loop(count // 256, body)
 
-    def widened(source, out):
+    def widened(source, start, here, base, count, step):
         def body(index):
-            at = rows_at(index * BLOCK, BLOCK)
-            out[at, :] = source[at, :].astype(F32)
-
-        loop(ROWS // BLOCK, body)
-
-    widened(block_in, block_out)
-    widened(grad_in, input_grad)
-    down_a[0] = shard_early[pl.ds(0, UNITS), :].astype(F32)
-    turned(shard_early, UNITS, up_b, UNITS)
-    out_a[0] = shard_late[pl.ds(0, CTX), :].astype(F32)
-    turned(shard_late, CTX, qkv_b, QKV)
-    up_a[0] = whole_early[pl.ds(0, WIDTH), :].astype(F32)
-    turned(whole_early, WIDTH, out_b, WIDTH)
-    turned(whole_late, 0, down_b, WIDTH)
-    qkv_a[0] = whole_late[pl.ds(WIDTH, WIDTH), :].astype(F32)
+            here[rows_at(base + index * step, step), :] = source[rows_at(start + index * step, step), :].astype(F32)
+
+        loop(count // step, body)
+
+    widened(block_in, 0, block_here, 0, ROWS, BLOCK)
+    send(block_here, block_out)
+    widened(grad_in, 0, grad_here, 0, ROWS, BLOCK)
+    send(grad_here, input_grad)
+    base = 0
+    for source, start, out, count in (
+        (whole_early, 0, up_a, WIDTH),
+        (whole_late, WIDTH, qkv_a, WIDTH),
+        (shard_early, 0, down_a, UNITS),
+        (shard_late, 0, out_a, CTX),
+    ):
+        widened(source, start, a_here, base, count, 256)
+        send(a_here.at[pl.ds(base, count)], out.at[0])
+        base += count
+    base = 0
+    for source, start, out, count in (
+        (whole_early, WIDTH, out_b, WIDTH),
+        (whole_late, 0, down_b, WIDTH),
+        (shard_early, UNITS, up_b, UNITS),
+        (shard_late, CTX, qkv_b, QKV),
+    ):
+        turned(source, start, base, count)
+        send(b_here.at[:, pl.ds(base, count)], out.at[0])
+        base += count
+    for copy in copies:
+        copy.wait()
 
 
 def finish_call(ins):
@@ -1325,7 +1407,12 @@
             shape(1, LANES, WIDTH, kind=F32),
         ],
         in_specs=[IN_VMEM] * 6,
-        out_specs=[IN_VMEM] * 10,
+        out_specs=[ANYWHERE] * 10,
+        scratch_shapes=[
+            pltpu.VMEM((ROWS, WIDTH), F32), pltpu.VMEM((ROWS, WIDTH), F32),
+            pltpu.VMEM((2 * WIDTH + UNITS + CTX, LANES), F32), pltpu.VMEM((LANES, 2 * WIDTH + UNITS + QKV), F32),
+            pltpu.SemaphoreType.DMA((10,)),
+        ],
         compiler_params=pltpu.CompilerParams(vmem_limit_bytes=VMEM_LIMIT),
     )(*ins)
 
@@ -1354,14 +1441,13 @@
             output_adapter_expand[0], gathered_grad, up_full, down_full,
         )
     )
-    block_own, input_own, shard_back, whole_back, shard_early, whole_early = back_call(
+    block_own, input_own, shard_early, shard_late, whole_early, whole_late = back_call(
         (
             grad_stage, output_full, qkv, tokens_own, first_norm_gain, mask_own, cot_own, down_offset_bias,
             down_adapter_expand[0], joined_adapter_reduce[0], normed_first, side_q, grad, middle, context,
             normed, side_u, side_o, shard_feed, joined_full, out_parts, probs,
         )
     )
-    shard_late, whole_late = reduce_call((shard_back, whole_back))
     return tuple(finish_call((shard_early, whole_early, shard_late, whole_late, block_own, input_own)))
 
 

time: 359 us -> 318 us (0.89)
  Pallas kernels: 352 us -> 314 us
    pallas_call x4 -> x3, Pallas kernels: 342 us -> 306 us  [call(): pl.pallas_call(kernel, name=kernel.__name__, out_shape=outs, in_specs=spe...]
where the time goes in v1:
time: 318 us; the launch traced here: 315 us
  Pallas kernels  314 us (99%)
    pallas_call x3, Pallas kernels, call(): pl.pallas_call(kernel, name=kernel.__name__, out_shape=outs, in_specs=spe...  306 us
    pallas_call x1, Pallas kernels, finish_call(): pl.pallas_call(finish_kernel, name='finish_kernel', out_shape=[shape(ROWS...  7.34 us

profile of v1, /device:TPU:1, one launch (start us, length us, event | category | flops | bytes accessed | tf_op | source)
XLA Modules:
  0.0 314.6 jit_solution(13703791494517006325)
XLA Ops:
  0.7 122.7 %forward_kernel.1 = (bf16[160,2176]{1,0:T(8,128)(2,1)}, f32[160,2048]{1,0:T(8,128)}, bf16[160,128]{1,0:T(8,128)(2,1)}, bf16[1280,256]{1,0:T(8,128)(2,1)}, bf16[1...) custom-call(f32[1,2048]{1,0:T(1,128)} %gain.5, ...), custom_call_target="tpu_custom_call" | custom-call | tf_op jit(solution)/shard_map/forward_kernel/pallas_call | solution.py:486
  123.4 69.0 %feed_kernel.1 = (f32[160,2048]{1,0:T(8,128)}, bf16[160,2176]{1,0:T(8,128)(2,1)}, bf16[160,128]{1,0:T(8,128)(2,1)}, bf16[2048,128]{1,0:T(8,128)(2,1)}, bf16[640,2176]{1,0:T(8,128)(2,1)}) custom-call(bf16[160,2176]{1,0:T(8,128)(2,1)} %get-tuple-element.38.normed.second_normed, f32[160,2048]{1,0:T(8,128)} %get-tuple-element.39.middle, ...), custom_call_target="tpu_custom_call" | custom-call | tf_op jit(solution)/shard_map/feed_kernel/pallas_call | solution.py:486
  192.4 114.4 %back_kernel.1 = (bf16[160,2048]{1,0:T(8,128)(2,1)}, bf16[160,2048]{1,0:T(8,128)(2,1)}, bf16[2048,128]{1,0:T(8,128)(2,1)}, bf16[1024,128]{1,0:T(8,128)(2,1)}, bf...) custom-call(bf16[160,2176]{1,0:T(8,128)(2,1)} %get-tuple-element.45.grad_stage, ...), custom_call_target="tpu_custom_call" | custom-call | tf_op jit(solution)/shard_map/back_kernel/pallas_call | solution.py:486
  306.8 7.3 %finish_kernel.1 = (f32[160,2048]{1,0:T(8,128)}, f32[160,2048]{1,0:T(8,128)}, f32[1,2048,128]{2,1,0:T(8,128)}, f32[1,128,768]{2,1,0:T(8,128)}, f32[1,256,128]{2,...) custom-call(bf16[2048,128]{1,0:T(8,128)(2,1)} %get-tuple-element.60., ...), custom_call_target="tpu_custom_call" | custom-call | tf_op jit(solution)/shard_map/finish_kernel/pallas_call | solution.py:1400

commit v2 on v1

--- a/solution.py
+++ b/solution.py
@@ -774,12 +774,43 @@
     )
 
 
+class SideSum:
+    def __init__(self, place, part, landing, send, recv):
+        self.place, self.part, self.landing = place, part, landing
+        self.copies = []
+        for k in range(1, 8):
+            y = lax.rem(place.y + k // 2, 4)
+            core = place.c if k % 2 == 0 else 1 - place.c
+            piece = part.at[rows_at((y * 2 + core) * ROWS, ROWS)]
+            self.copies.append(remote(piece, landing.at[k], send.at[k], recv.at[k], place.at(y=y, c=core)))
+
+    def open(self):
+        for copy in self.copies:
+            copy.start()
+
+    def total(self):
+        total = self.part[rows_at(self.place.ring(0, True) * ROWS, ROWS), :].astype(F32)
+        for k in range(1, 8):
+            self.copies[k - 1].wait_recv()
+            total = total + self.landing[k].astype(F32)
+        return total
+
+    def end(self):
+        for copy in self.copies:
+            copy.wait_send()
+
+
+def side_scratch():
+    dma = pltpu.SemaphoreType.DMA
+    return [pltpu.VMEM((GROUP, LANES), BF), pltpu.VMEM((8, ROWS, LANES), BF), dma((8,)), dma((8,))]
+
+
 def feed_kernel(
     normed, middle, up_shift, mask, gain, up_reduce, output_expand,
     gathered_grad, up_weights, down_weights,
-    grad_out, grad_stage, side_u, by_shard, out_parts,
+    grad_out, grad_stage, side_u, side_d, by_shard, out_parts,
     up_full, down_full, grads, rows, rows_send, rows_recv, act, slope, part, sib_in, relay, near, s_send, s_recv,
-    part_out, sib_in_out, t_send, t_recv, own_sem,
+    part_out, sib_in_out, t_send, t_recv, side_part, side_in, side_send, side_recv, own_sem,
 ):
     p = Place()
     own_rows = rows_at(p.ring(0, True) * ROWS, ROWS)
@@ -791,7 +822,7 @@
     load_grads.start()
     load_up = pltpu.make_async_copy(up_weights, up_full, own_sem.at[3])
     load_up.start()
-    greet([p.sib, p.up, p.down])
+    greet(p.ring_mates())
     gather = Gather(p, rows, rows_send, rows_recv)
     stage.wait()
     gather.begin()
@@ -828,10 +859,11 @@
     def forth(dy):
         at = pair_rows(p, dy)
 
-        def put(lanes, value):
-            part_out[at, lanes] = value.astype(BF)
-
-        wide_product(put, lambda lanes: nn(act[at, :], down_full[:, lanes]))
+        def body(j):
+            lanes = lanes_at(j * 512, 512)
+            part_out[at, lanes] = nn(act[at, :], down_full[:, lanes]).astype(BF)
+
+        loop(WIDTH // 512, body)
 
     load_down.wait()
     load_grads.wait()
@@ -868,6 +900,9 @@
     scatter_out.exchange(2)
     scatter.near_rest()
     scatter.combine(0)
+    side_part[...] = nn(act[...], down_full[:, pl.ds(WIDTH, LANES)]).astype(BF)
+    side = SideSum(p, side_part, side_in, side_send, side_recv)
+    side.open()
     for dy in (1, -1, 0):
         forth(dy)
         scatter_out.exchange(dy)
@@ -880,6 +915,7 @@
         ).astype(BF)
 
     loop(UNITS // 256, by_unit)
+    mask_rows = mask[...].astype(F32)
     for dy in range(4):
         scatter_out.combine(dy)
     copies = []
@@ -892,7 +928,6 @@
     for dy in range(4):
         hand_on(scatter_out.mine(dy), dy * ROWS, ROWS)
     scatter.arrived()
-    mask_rows = mask[...].astype(F32)
     side_u[...] = (mask_rows * scatter.total(0, ROWS, pl.ds(WIDTH, LANES))).astype(BF)
 
     def norm_block(index):
@@ -907,7 +942,9 @@
     grad_stage[:, pl.ds(WIDTH, LANES)] = (
         mask_rows * (SCALE * nt(grad_stage[:, pl.ds(0, WIDTH)], output_expand[...]))
     ).astype(BF)
+    side_d[...] = (mask_rows * side.total()).astype(BF)
     gather.end()
+    side.end()
     scatter.end()
     scatter_out.end(0, 4)
     for copy in copies:
@@ -916,21 +953,21 @@
 
 def feed_call(ins):
     outs = [
-        shape(ROWS, WIDTH, kind=F32), shape(ROWS, WIDE), shape(ROWS, LANES), shape(2 * UNITS, LANES),
-        shape(4 * ROWS, WIDE),
+        shape(ROWS, WIDTH, kind=F32), shape(ROWS, WIDE), shape(ROWS, LANES), shape(ROWS, LANES),
+        shape(2 * UNITS, LANES), shape(4 * ROWS, WIDTH),
     ]
-    scratch = scatter_scratch()
+    scratch = scatter_scratch(WIDTH)
     return call(
         feed_kernel,
         2,
         ins,
         [IN_VMEM] * 7 + [ANYWHERE] * 3,
         outs,
-        [IN_VMEM] * 4 + [ANYWHERE],
+        [IN_VMEM] * 5 + [ANYWHERE],
         [
             pltpu.VMEM((WIDE, UNITS), BF), pltpu.VMEM((UNITS, WIDE), BF), pltpu.VMEM((GROUP, WIDE), BF),
-            *gather_scratch(), pltpu.VMEM((GROUP, UNITS), BF), pltpu.VMEM((GROUP, UNITS), BF), *scratch,
-            scratch[0], scratch[1], scratch[4], scratch[5], pltpu.SemaphoreType.DMA((8,)),
+            *gather_scratch(), pltpu.VMEM((GROUP, UNITS), BF), pltpu.VMEM((GROUP, UNITS), BF), *scatter_scratch(),
+            scratch[0], scratch[1], scratch[4], scratch[5], *side_scratch(), pltpu.SemaphoreType.DMA((8,)),
         ],
     )
 
@@ -1106,46 +1143,125 @@
         super().close()
 
 
+class PlaneSum(Reducer):
+    def __init__(self, place, source, refs):
+        (
+            self.landing, self.slice_sum, self.bits_in, self.bit_sum, self.all,
+            self.b_send, self.b_recv, self.d_send, self.d_recv, self.e_send, self.e_recv, self.g_send, self.g_recv,
+            self.mark,
+        ) = refs
+        super().__init__(place, source, self.b_send.at[0])
+        self.q = self.m * 2 + place.c
+        self.slice = source.shape[0] // 32
+        self.bit = self.slice // 4
+        self.base = self.q * self.slice
+
+    @staticmethod
+    def scratch(count):
+        dma = pltpu.SemaphoreType.DMA
+        piece = count // 32
+        return [
+            pltpu.VMEM((32, piece, LANES), BF), pltpu.VMEM((piece, LANES), BF), pltpu.VMEM((4, piece // 4, LANES), BF),
+            pltpu.VMEM((piece // 4, LANES), BF), pltpu.VMEM((count, LANES), BF),
+            dma((32,)), dma((32,)), dma((4,)), dma((4,)), dma((4,)), dma((4,)), dma((32,)), dma((32,)), dma((1,)),
+        ]
+
+    def mate(self, k):
+        other = lax.rem(self.q + k, 32)
+        m = lax.div(other, 2)
+        return other, self.p.at(z=lax.div(m, 4), x=lax.rem(m, 4), c=lax.rem(other, 2))
+
+    def open(self):
+        for k in range(1, 32):
+            other, device = self.mate(k)
+            piece = self.source.at[rows_at(other * self.slice, self.slice)]
+            self.push(piece, self.landing.at[k], self.b_send.at[k], self.b_recv.at[k], device)
+
+    def slices(self):
+        total = self.source[rows_at(self.base, self.slice), :].astype(F32)
+        for k in range(1, 32):
+            self.await_at(self.landing.at[k], self.b_recv.at[k])
+            total = total + self.landing[k].astype(F32)
+        self.slice_sum[...] = total.astype(BF)
+        for dy in (2, 1, 3):
+            other = lax.rem(self.p.y + dy, 4)
+            piece = self.slice_sum.at[rows_at(other * self.bit, self.bit)]
+            self.push(piece, self.bits_in.at[dy], self.d_send.at[dy], self.d_recv.at[dy], self.p.at(y=other))
+
+    def bits(self):
+        total = self.slice_sum[rows_at(self.p.y * self.bit, self.bit), :].astype(F32)
+        for dy in (1, 3, 2):
+            self.await_at(self.bits_in.at[dy], self.d_recv.at[dy])
+            total = total + self.bits_in[dy].astype(F32)
+        self.bit_sum[...] = total.astype(BF)
+        own = self.all.at[rows_at(self.base + self.p.y * self.bit, self.bit)]
+        self.placed = pltpu.make_async_copy(self.bit_sum, own, self.mark.at[0])
+        self.placed.start()
+        for dy in (2, 1, 3):
+            device = self.p.at(y=lax.rem(self.p.y + dy, 4))
+            self.push(self.bit_sum, own, self.e_send.at[dy], self.e_recv.at[dy], device)
+
+    def slices_back(self):
+        self.placed.wait()
+        for dy in (1, 3, 2):
+            source = lax.rem(self.p.y + 4 - dy, 4)
+            self.await_at(self.all.at[rows_at(self.base + source * self.bit, self.bit)], self.e_recv.at[dy])
+        own = self.all.at[rows_at(self.base, self.slice)]
+        for k in range(1, 32):
+            self.push(own, own, self.g_send.at[k], self.g_recv.at[k], self.mate(k)[1])
+
+    def close(self):
+        for k in range(1, 32):
+            source = lax.rem(self.q + 32 - k, 32)
+            self.await_at(self.all.at[rows_at(source * self.slice, self.slice)], self.g_recv.at[k])
+        super().close()
+
+
 def back_kernel(
-    grad_stage, output_full, qkv, tokens, gain, mask, cotangent, down_shift, down_expand, joined_reduce, normed, side_q,
-    grad, middle, context, second_normed, side_u, side_o, shard_early,
-    joined_weights, out_parts, probs_in,
+    gain, mask, down_shift, side_u, side_o, side_d,
+    grad_stage_in, output_in, qkv_in, context_in, tokens_in, cotangent_in, down_expand_in, joined_reduce_in, normed_in,
+    side_q_in, grad_in, middle_in, second_in, shard_in, joined_in, out_parts, probs_in,
     block_out, input_grad, shard_done, shard_rest, whole_done, whole_rest,
-    rows, rows_send, rows_recv, probs, key_grad, value_grad, joined_grad, result, block_own, joined_full, whole_early,
-    shard_late, whole_late, side_part, side_in, side_send, side_recv,
-    part, sib_in, relay, near, s_send, s_recv, parts, relay_out, near_out, t_send, t_recv, swap_send, swap_recv, own_sem,
+    grad_stage, output_full, qkv, context, tokens, cotangent, down_expand, joined_reduce, normed, side_q, grad, middle,
+    second_normed, shard_early, joined_full, parts, probs, load_sem,
+    rows, rows_send, rows_recv, key_grad, value_grad, joined_grad, result, block_own, whole_early, shard_late,
+    whole_late, side_part, side_in, side_send, side_recv,
+    part, sib_in, relay, near, s_send, s_recv, relay_out, near_out, t_send, t_recv, swap_send, swap_recv,
     *refs,
 ):
     p = Place()
     own_rows = rows_at(p.ring(0, True) * ROWS, ROWS)
-    loads = []
-
-    def load(src, dst):
-        copy = pltpu.make_async_copy(src, dst, own_sem.at[len(loads)])
+    sources = (
+        grad_stage_in, shard_in, second_in, cotangent_in, output_in, qkv_in, context_in, probs_in, out_parts, joined_in,
+        side_q_in, normed_in, joined_reduce_in, middle_in, down_expand_in, grad_in, tokens_in,
+    )
+    targets = (
+        grad_stage, shard_early, second_normed, cotangent, output_full, qkv, context, probs, parts, joined_full,
+        side_q, normed, joined_reduce, middle, down_expand, grad, tokens,
+    )
+    loads = [pltpu.make_async_copy(src, dst, load_sem.at[i]) for i, (src, dst) in enumerate(zip(sources, targets))]
+    stage = pltpu.make_async_copy(grad_stage_in, rows.at[own_rows], load_sem.at[17])
+    stage.start()
+    for copy in loads:
         copy.start()
-        loads.append(copy)
-
-    load(grad_stage, rows.at[own_rows])
-    for dy in (0, 1, -1, 2):
-        at = pair_rows(p, dy)
-        load(probs_in.at[:, at], probs.at[:, at])
-    load(out_parts, parts)
-    load(joined_weights, joined_full)
     greet(p.ring_mates() + Reducer.mates(p))
     gather = Gather(p, rows, rows_send, rows_recv)
-    loads[0].wait()
+    stage.wait()
     gather.begin()
     swap = Swap(p, [(block_own, block_out), (result, input_grad)], swap_send, swap_recv)
     early_shard = ShardSum(p, shard_early, refs[0:7])
     early_whole = WholeSum(p, whole_early, refs[7:25])
     late_shard = ShardSum(p, shard_late, refs[25:32])
-    late_whole = WholeSum(p, whole_late, refs[32:50])
+    late_whole = PlaneSum(p, whole_late, refs[32:46])
+    for copy in loads[:4]:
+        copy.wait()
     early_shard.open()
 
     def early_column(j):
         lanes = lanes_at(j * 256, 256)
         whole_early[lanes, :] = tn(second_normed[:, lanes], side_u[...]).astype(BF)
         whole_early[lanes_at(WIDTH + j * 256, 256), :] = (SCALE * tn(grad_stage[:, lanes], side_o[...])).astype(BF)
+        whole_early[lanes_at(2 * WIDTH + j * 256, 256), :] = (SCALE * tn(cotangent[:, lanes], side_d[...])).astype(BF)
 
     loop(WIDTH // 256, early_column)
     early_whole.open()
@@ -1177,27 +1293,24 @@
     key_grad[...] = jnp.zeros_like(key_grad)
     scatter_out = Scatter(p, parts, None, relay_out, near_out, t_send, t_recv, lambda dy: dy % 4 * ROWS)
     gather.own_pair()
-    loads[1].wait()
+    for copy in loads[4:8]:
+        copy.wait()
     back(0)
     early_whole.halves()
-    loads[5].wait()
+    loads[8].wait()
     gather.near()
     scatter_out.relay_out()
     scatter_out.near_free(1)
     scatter_out.near_free(-1)
     gather.near_pairs()
-    loads[2].wait()
     back(1)
     gather.far()
     early_shard.spread()
-    loads[3].wait()
     back(-1)
     early_whole.slices()
     gather.far_pair()
     scatter_out.near_rest()
-    loads[4].wait()
     back(2)
-    early_whole.bits()
     turn = identity()
     for head in range(2):
         start = head * 3 * HEAD
@@ -1205,7 +1318,8 @@
             (key_grad[head] * (1.0 / math.sqrt(HEAD))).astype(BF), turn
         ).astype(BF)
         joined_grad[:, start + 2 * HEAD : start + 3 * HEAD] = tn(value_grad[head].astype(BF), turn).astype(BF)
-    loads[6].wait()
+    for copy in loads[9:]:
+        copy.wait()
 
     def product(dy):
         at = pair_rows(p, dy)
@@ -1220,46 +1334,31 @@
     product(2)
     scatter.exchange(2)
     side_part[...] = nt(joined_grad[...], joined_full[pl.ds(WIDTH, LANES), :]).astype(BF)
-    side_copies = []
-    for k in range(1, 8):
-        dy, same = k // 2, k % 2 == 0
-        y, core = lax.rem(p.y + dy, 4), (p.c if same else 1 - p.c)
-        copy = remote(
-            side_part.at[rows_at((y * 2 + core) * ROWS, ROWS)], side_in.at[k], side_send.at[k], side_recv.at[k],
-            p.at(y=y, c=core),
-        )
-        copy.start()
-        side_copies.append(copy)
+    side = SideSum(p, side_part, side_in, side_send, side_recv)
+    side.open()
+    early_whole.bits()
     scatter.combine(2)
     scatter.relay_out()
     product(1)
     scatter.exchange(1)
+    mask_rows = mask[...].astype(F32)
+    side_part[own_rows, :] = (mask_rows * side.total()).astype(BF)
+
+    def late_column(j):
+        lanes = lanes_at(j * 256, 256)
+        whole_late[lanes, :] = tn(normed[:, lanes], side_part[own_rows, :]).astype(BF)
+
+    loop(WIDTH // 256, late_column)
+    late_whole.open()
     product(-1)
     scatter.exchange(-1)
     scatter.combine(1)
     scatter.near_free(1)
+    product(0)
+    scatter.exchange(0)
     scatter.combine(-1)
     scatter.near_free(-1)
-    mask_rows = mask[...].astype(F32)
-    side_total = side_part[own_rows, :].astype(F32)
-    for k in range(1, 8):
-        side_copies[k - 1].wait_recv()
-        side_total = side_total + side_in[k].astype(F32)
-    side_part[own_rows, :] = (mask_rows * side_total).astype(BF)
-    scatter_out.arrived()
-    side_d = (mask_rows * scatter_out.total(0, ROWS, pl.ds(WIDTH, LANES))).astype(BF)
-
-    def late_column(j):
-        lanes = lanes_at(j * 256, 256)
-        whole_late[lanes, :] = (SCALE * tn(cotangent[:, lanes], side_d)).astype(BF)
-        whole_late[lanes_at(WIDTH + j * 256, 256), :] = tn(normed[:, lanes], side_part[own_rows, :]).astype(BF)
-
-    loop(WIDTH // 256, late_column)
-    late_whole.open()
-    product(0)
-    scatter.exchange(0)
     scatter.near_rest()
-    late_whole.halves()
     scatter.combine(0)
     shard_late[pl.ds(0, CTX), :] = tn(context[...], rows[:, pl.ds(WIDTH, LANES)]).astype(BF)
 
@@ -1269,7 +1368,7 @@
 
     loop(QKV // 256, late_lane)
     late_shard.open()
-    early_whole.slices_back()
+    scatter_out.arrived()
 
     def add_tile(j):
         lanes = lanes_at(j * 256, 256)
@@ -1277,12 +1376,13 @@
             middle[:, lanes]
             + scatter_out.total(0, ROWS, lanes)
             + down_shift[:, lanes]
-            + SCALE * nn(side_d, down_expand[:, lanes])
+            + SCALE * nn(side_d[...], down_expand[:, lanes])
         ).astype(BF)
 
     loop(WIDTH // 256, add_tile)
     swap.begin(0)
     late_whole.slices()
+    early_whole.slices_back()
     late_shard.spread()
     late_whole.bits()
     late_whole.slices_back()
@@ -1290,14 +1390,13 @@
 
     def norm_block(index):
         at = rows_at(index * BLOCK, BLOCK)
-        side = side_part[rows_at(p.ring(0, True) * ROWS + index * BLOCK, BLOCK), :]
-        back_grad = scatter.total(index * BLOCK, BLOCK, pl.ds(0, WIDTH)) + nt(side, joined_reduce[...])
+        side_rows = side_part[rows_at(p.ring(0, True) * ROWS + index * BLOCK, BLOCK), :]
+        back_grad = scatter.total(index * BLOCK, BLOCK, pl.ds(0, WIDTH)) + nt(side_rows, joined_reduce[...])
         result[at, :] = (grad[at, :] + norm_back(tokens[at, :].astype(F32), gain[...], back_grad)).astype(BF)
 
     loop(ROWS // BLOCK, norm_block)
     swap.begin(1)
     early_whole.halves_back()
-    late_whole.halves_back()
     early_shard.close()
     late_shard.close()
     early_whole.close()
@@ -1309,8 +1408,7 @@
     gather.end()
     scatter.end()
     scatter_out.end(4)
-    for copy in side_copies:
-        copy.wait_send()
+    side.end()
     swap.arrived(0)
     swap.arrived(1)
     swap.end()
@@ -1319,26 +1417,28 @@
 def back_call(ins):
     outs = [
         shape(ROWS, WIDTH), shape(ROWS, WIDTH), shape(2 * UNITS, LANES), shape(CTX + QKV, LANES),
-        shape(2 * WIDTH, LANES), shape(2 * WIDTH, LANES),
+        shape(3 * WIDTH, LANES), shape(WIDTH, LANES),
     ]
     dma = pltpu.SemaphoreType.DMA
-    scratch = scatter_scratch()
+    vmem = pltpu.VMEM
     return call(
         back_kernel,
         3,
         ins,
-        [IN_VMEM] * 19 + [ANYWHERE] * 3,
+        [IN_VMEM] * 6 + [ANYWHERE] * 17,
         outs,
         [ANYWHERE] * 2 + [IN_VMEM] * 4,
         [
-            *gather_scratch(), pltpu.VMEM((2, GROUP, GROUP), BF), pltpu.VMEM((2, HEAD, GROUP), F32),
-            pltpu.VMEM((2, HEAD, GROUP), F32), pltpu.VMEM((GROUP, QKV), BF), pltpu.VMEM((ROWS, WIDTH), BF),
-            pltpu.VMEM((ROWS, WIDTH), BF), pltpu.VMEM((WIDE, QKV), BF), pltpu.VMEM((2 * WIDTH, LANES), BF),
-            pltpu.VMEM((CTX + QKV, LANES), BF), pltpu.VMEM((2 * WIDTH, LANES), BF), pltpu.VMEM((GROUP, LANES), BF),
-            pltpu.VMEM((8, ROWS, LANES), BF), dma((8,)), dma((8,)), *scatter_scratch(WIDTH),
-            pltpu.VMEM((4 * ROWS, WIDE), BF), *scratch[2:], *swap_marks(2), dma((7,)),
-            *ShardSum.scratch(2 * UNITS), *WholeSum.scratch(2 * WIDTH), *ShardSum.scratch(CTX + QKV),
-            *WholeSum.scratch(2 * WIDTH),
+            vmem((ROWS, WIDE), BF), vmem((CTX, WIDE), BF), vmem((GROUP, QKV), BF), vmem((GROUP, CTX), BF),
+            vmem((ROWS, WIDTH), BF), vmem((ROWS, WIDTH), BF), vmem((LANES, WIDTH), BF), vmem((WIDTH, LANES), BF),
+            vmem((ROWS, WIDTH), BF), vmem((GROUP, LANES), BF), vmem((ROWS, WIDTH), F32), vmem((ROWS, WIDTH), F32),
+            vmem((ROWS, WIDE), BF), vmem((2 * UNITS, LANES), BF), vmem((WIDE, QKV), BF), vmem((4 * ROWS, WIDTH), BF),
+            vmem((2, GROUP, GROUP), BF), dma((18,)),
+            *gather_scratch(), vmem((2, HEAD, GROUP), F32), vmem((2, HEAD, GROUP), F32), vmem((GROUP, QKV), BF),
+            vmem((ROWS, WIDTH), BF), vmem((ROWS, WIDTH), BF), vmem((3 * WIDTH, LANES), BF),
+            vmem((CTX + QKV, LANES), BF), vmem((WIDTH, LANES), BF), *side_scratch(), *scatter_scratch(WIDTH),
+            *scatter_scratch(WIDTH)[2:], *swap_marks(2), *ShardSum.scratch(2 * UNITS), *WholeSum.scratch(3 * WIDTH),
+            *ShardSum.scratch(CTX + QKV), *PlaneSum.scratch(WIDTH),
         ],
     )
 
@@ -1375,7 +1475,7 @@
     base = 0
     for source, start, out, count in (
         (whole_early, 0, up_a, WIDTH),
-        (whole_late, WIDTH, qkv_a, WIDTH),
+        (whole_late, 0, qkv_a, WIDTH),
         (shard_early, 0, down_a, UNITS),
         (shard_late, 0, out_a, CTX),
     ):
@@ -1385,7 +1485,7 @@
     base = 0
     for source, start, out, count in (
         (whole_early, WIDTH, out_b, WIDTH),
-        (whole_late, 0, down_b, WIDTH),
+        (whole_early, 2 * WIDTH, down_b, WIDTH),
         (shard_early, UNITS, up_b, UNITS),
         (shard_late, CTX, qkv_b, QKV),
     ):
@@ -1435,7 +1535,7 @@
             up_matrix[0], up_adapter_expand[0], down_matrix[0], down_adapter_reduce[0],
         )
     )
-    grad, grad_stage, side_u, shard_feed, out_parts = feed_call(
+    grad, grad_stage, side_u, side_d, shard_feed, out_parts = feed_call(
         (
             normed, middle, up_shift_own, mask_own, second_norm_gain, up_adapter_reduce[0],
             output_adapter_expand[0], gathered_grad, up_full, down_full,
@@ -1443,9 +1543,9 @@
     )
     block_own, input_own, shard_early, shard_late, whole_early, whole_late = back_call(
         (
-            grad_stage, output_full, qkv, tokens_own, first_norm_gain, mask_own, cot_own, down_offset_bias,
-            down_adapter_expand[0], joined_adapter_reduce[0], normed_first, side_q, grad, middle, context,
-            normed, side_u, side_o, shard_feed, joined_full, out_parts, probs,
+            first_norm_gain, mask_own, down_offset_bias, side_u, side_o, side_d, grad_stage, output_full, qkv, context,
+            tokens_own, cot_own, down_adapter_expand[0], joined_adapter_reduce[0], normed_first, side_q, grad, middle,
+            normed, shard_feed, joined_full, out_parts, probs,
         )
     )
     return tuple(finish_call((shard_early, whole_early, shard_late, whole_late, block_own, input_own)))

time: 318 us -> 313 us (0.984)
  Pallas kernels: 314 us -> 308 us
    pallas_call x3, Pallas kernels: 306 us -> 301 us  [call(): pl.pallas_call(kernel, name=kernel.__name__, out_shape=outs, in_specs=spe...]
where the time goes in v2:
time: 313 us; the launch traced here: 309 us
  Pallas kernels  308 us (98%)
    pallas_call x3, Pallas kernels, call(): pl.pallas_call(kernel, name=kernel.__name__, out_shape=outs, in_specs=spe...  301 us
    pallas_call x1, Pallas kernels, finish_call(): pl.pallas_call(finish_kernel, name='finish_kernel', out_shape=[shape(ROWS...  7.34 us

profile of v2, /device:TPU:1, one launch (start us, length us, event | category | flops | bytes accessed | tf_op | source)
XLA Modules:
  0.0 309.4 jit_solution(6850450213981225508)
XLA Ops:
  0.7 122.7 %forward_kernel.1 = (bf16[160,2176]{1,0:T(8,128)(2,1)}, f32[160,2048]{1,0:T(8,128)}, bf16[160,128]{1,0:T(8,128)(2,1)}, bf16[1280,256]{1,0:T(8,128)(2,1)}, bf16[1...) custom-call(f32[1,2048]{1,0:T(1,128)} %gain.5, ...), custom_call_target="tpu_custom_call" | custom-call | tf_op jit(solution)/shard_map/forward_kernel/pallas_call | solution.py:486
  123.4 71.0 %feed_kernel.1 = (f32[160,2048]{1,0:T(8,128)}, bf16[160,2176]{1,0:T(8,128)(2,1)}, bf16[160,128]{1,0:T(8,128)(2,1)}, bf16[160,128]{1,0:T(8,128)(2,1)}, bf16[2048,...) custom-call(bf16[160,2176]{1,0:T(8,128)(2,1)} %get-tuple-element.40.normed.second_in, ...), custom_call_target="tpu_custom_call" | custom-call | tf_op jit(solution)/shard_map/feed_kernel/pallas_call | solution.py:486
  194.4 107.1 %back_kernel.1 = (bf16[160,2048]{1,0:T(8,128)(2,1)}, bf16[160,2048]{1,0:T(8,128)(2,1)}, bf16[2048,128]{1,0:T(8,128)(2,1)}, bf16[1024,128]{1,0:T(8,128)(2,1)}, bf...) custom-call(f32[1,2048]{1,0:T(1,128)} %gain.5, bf16[160,128]{1,0:T(8,128)(2,1)} %get-tuple-element.39.mask, ...), custom_call_target="tpu_custom_call" | custom-call | tf_op jit(solution)/shard_map/back_kernel/pallas_call | solution.py:486
  301.6 7.3 %finish_kernel.1 = (f32[160,2048]{1,0:T(8,128)}, f32[160,2048]{1,0:T(8,128)}, f32[1,2048,128]{2,1,0:T(8,128)}, f32[1,128,768]{2,1,0:T(8,128)}, f32[1,256,128]{2,...) custom-call(bf16[2048,128]{1,0:T(8,128)(2,1)} %get-tuple-element.62., ...), custom_call_target="tpu_custom_call" | custom-call | tf_op jit(solution)/shard_map/finish_kernel/pallas_call | solution.py:1500

commit v3 on v2

--- a/solution.py
+++ b/solution.py
@@ -78,6 +78,7 @@
         self.z_up = self.at(z=lax.rem(self.z + 1, 4))
         self.z_down = self.at(z=lax.rem(self.z + 3, 4))
         self.partner = self.at(g=self.c, c=self.g)
+        self.beside = self.at(x=lax.rem(self.x + 2 * self.xl + 3, 4), c=self.g)
         self.home = self.c == self.g
         self.away = self.c != self.g
 
@@ -430,8 +431,8 @@
 
 
 class Swap:
-    def __init__(self, place, pairs, send, recv):
-        self.place, self.pairs, self.send, self.recv = place, pairs, send, recv
+    def __init__(self, place, pairs, send, recv, shared=()):
+        self.place, self.pairs, self.send, self.recv, self.shared = place, pairs, send, recv, shared
 
     def begin(self, i):
         src, dst = self.pairs[i]
@@ -443,7 +444,8 @@
 
         @pl.when(p.away)
         def _():
-            remote(src, dst, self.send.at[i], self.recv.at[i], p.partner).start()
+            device = p.beside if i in self.shared else p.partner
+            remote(src, dst, self.send.at[i], self.recv.at[i], device).start()
 
     def arrived(self, i):
         src, dst = self.pairs[i]
@@ -560,6 +562,7 @@
         ],
         swap_send,
         swap_recv,
+        (2, 3, 5, 6, 7, 8),
     )
     joined.first()
     swap.begin(0)
@@ -879,22 +882,22 @@
     gather.near_pairs()
     hide(1)
     hide(-1)
-    gather.far()
-    gather.far_pair()
-    hide(2)
-    back(2)
-    scatter.exchange(2)
     back(1)
     scatter.exchange(1)
-    scatter.combine(2)
-    scatter.relay_out()
+    gather.far()
     back(-1)
     scatter.exchange(-1)
+    gather.far_pair()
     scatter.combine(1)
     scatter.near_free(1)
     scatter.combine(-1)
     scatter.near_free(-1)
+    hide(2)
+    back(2)
+    scatter.exchange(2)
     back(0)
+    scatter.combine(2)
+    scatter.relay_out()
     scatter.exchange(0)
     forth(2)
     scatter_out.exchange(2)

time: 313 us -> 311 us (level)
  no operation moved by 1% of the time
where the time goes in v3:
time: 311 us; the launch traced here: 308 us
  Pallas kernels  307 us (99%)
    pallas_call x3, Pallas kernels, call(): pl.pallas_call(kernel, name=kernel.__name__, out_shape=outs, in_specs=spe...  300 us
    pallas_call x1, Pallas kernels, finish_call(): pl.pallas_call(finish_kernel, name='finish_kernel', out_shape=[shape(ROWS...  7.34 us

profile of v3, /device:TPU:1, one launch (start us, length us, event | category | flops | bytes accessed | tf_op | source)
XLA Modules:
  0.0 308.2 jit_solution(14099213026537454650)
XLA Ops:
  0.7 122.5 %forward_kernel.1 = (bf16[160,2176]{1,0:T(8,128)(2,1)}, f32[160,2048]{1,0:T(8,128)}, bf16[160,128]{1,0:T(8,128)(2,1)}, bf16[1280,256]{1,0:T(8,128)(2,1)}, bf16[1...) custom-call(f32[1,2048]{1,0:T(1,128)} %gain.5, ...), custom_call_target="tpu_custom_call" | custom-call | tf_op jit(solution)/shard_map/forward_kernel/pallas_call | solution.py:488
  123.1 68.9 %feed_kernel.1 = (f32[160,2048]{1,0:T(8,128)}, bf16[160,2176]{1,0:T(8,128)(2,1)}, bf16[160,128]{1,0:T(8,128)(2,1)}, bf16[160,128]{1,0:T(8,128)(2,1)}, bf16[2048,...) custom-call(bf16[160,2176]{1,0:T(8,128)(2,1)} %get-tuple-element.40.normed.second_in, ...), custom_call_target="tpu_custom_call" | custom-call | tf_op jit(solution)/shard_map/feed_kernel/pallas_call | solution.py:488
  192.1 108.3 %back_kernel.1 = (bf16[160,2048]{1,0:T(8,128)(2,1)}, bf16[160,2048]{1,0:T(8,128)(2,1)}, bf16[2048,128]{1,0:T(8,128)(2,1)}, bf16[1024,128]{1,0:T(8,128)(2,1)}, bf...) custom-call(f32[1,2048]{1,0:T(1,128)} %gain.5, bf16[160,128]{1,0:T(8,128)(2,1)} %get-tuple-element.39.mask, ...), custom_call_target="tpu_custom_call" | custom-call | tf_op jit(solution)/shard_map/back_kernel/pallas_call | solution.py:488
  300.4 7.3 %finish_kernel.1 = (f32[160,2048]{1,0:T(8,128)}, f32[160,2048]{1,0:T(8,128)}, f32[1,2048,128]{2,1,0:T(8,128)}, f32[1,128,768]{2,1,0:T(8,128)}, f32[1,256,128]{2,...) custom-call(bf16[2048,128]{1,0:T(8,128)(2,1)} %get-tuple-element.62., ...), custom_call_target="tpu_custom_call" | custom-call | tf_op jit(solution)/shard_map/finish_kernel/pallas_call | solution.py:1503

commit v4 on v3

--- a/solution.py
+++ b/solution.py
@@ -1447,10 +1447,18 @@
 
 
 def finish_kernel(
-    shard_early, whole_early, shard_late, whole_late, block_in, grad_in,
+    shard_early_in, whole_early_in, shard_late_in, whole_late_in, block_from, grad_from,
     block_out, input_grad, qkv_a, qkv_b, out_a, out_b, up_a, up_b, down_a, down_b,
+    shard_early, whole_early, shard_late, whole_late, block_in, grad_in, load_sem,
     block_here, grad_here, a_here, b_here, out_sem,
 ):
+    loads = []
+    for src, dst in (
+        (block_from, block_in), (grad_from, grad_in), (whole_early_in, whole_early), (whole_late_in, whole_late),
+        (shard_early_in, shard_early), (shard_late_in, shard_late),
+    ):
+        loads.append(pltpu.make_async_copy(src, dst, load_sem.at[len(loads)]))
+        loads[-1].start()
     turn = identity()
     copies = []
 
@@ -1471,10 +1479,14 @@
 
         loop(count // step, body)
 
+    loads[0].wait()
     widened(block_in, 0, block_here, 0, ROWS, BLOCK)
     send(block_here, block_out)
+    loads[1].wait()
     widened(grad_in, 0, grad_here, 0, ROWS, BLOCK)
     send(grad_here, input_grad)
+    for load in loads[2:]:
+        load.wait()
     base = 0
     for source, start, out, count in (
         (whole_early, 0, up_a, WIDTH),
@@ -1509,10 +1521,12 @@
             shape(1, WIDTH, LANES, kind=F32), shape(1, LANES, UNITS, kind=F32), shape(1, UNITS, LANES, kind=F32),
             shape(1, LANES, WIDTH, kind=F32),
         ],
-        in_specs=[IN_VMEM] * 6,
+        in_specs=[ANYWHERE] * 6,
         out_specs=[ANYWHERE] * 10,
         scratch_shapes=[
-            pltpu.VMEM((ROWS, WIDTH), F32), pltpu.VMEM((ROWS, WIDTH), F32),
+            pltpu.VMEM((2 * UNITS, LANES), BF), pltpu.VMEM((3 * WIDTH, LANES), BF), pltpu.VMEM((CTX + QKV, LANES), BF),
+            pltpu.VMEM((WIDTH, LANES), BF), pltpu.VMEM((ROWS, WIDTH), BF), pltpu.VMEM((ROWS, WIDTH), BF),
+            pltpu.SemaphoreType.DMA((6,)), pltpu.VMEM((ROWS, WIDTH), F32), pltpu.VMEM((ROWS, WIDTH), F32),
             pltpu.VMEM((2 * WIDTH + UNITS + CTX, LANES), F32), pltpu.VMEM((LANES, 2 * WIDTH + UNITS + QKV), F32),
             pltpu.SemaphoreType.DMA((10,)),
         ],

time: 311 us -> 311 us (level)
  no operation moved by 1% of the time
where the time goes in v4:
time: 311 us; the launch traced here: 308 us
  Pallas kernels  307 us (99%)
    pallas_call x3, Pallas kernels, call(): pl.pallas_call(kernel, name=kernel.__name__, out_shape=outs, in_specs=spe...  300 us
    pallas_call x1, Pallas kernels, finish_call(): pl.pallas_call(finish_kernel, name='finish_kernel', out_shape=[shape(ROWS...  7.3 us

profile of v4, /device:TPU:1, one launch (start us, length us, event | category | flops | bytes accessed | tf_op | source)
XLA Modules:
  0.0 308.2 jit_solution(1935900330767070835)
XLA Ops:
  0.7 122.5 %forward_kernel.1 = (bf16[160,2176]{1,0:T(8,128)(2,1)}, f32[160,2048]{1,0:T(8,128)}, bf16[160,128]{1,0:T(8,128)(2,1)}, bf16[1280,256]{1,0:T(8,128)(2,1)}, bf16[1...) custom-call(f32[1,2048]{1,0:T(1,128)} %gain.5, ...), custom_call_target="tpu_custom_call" | custom-call | tf_op jit(solution)/shard_map/forward_kernel/pallas_call | solution.py:488
  123.1 68.9 %feed_kernel.1 = (f32[160,2048]{1,0:T(8,128)}, bf16[160,2176]{1,0:T(8,128)(2,1)}, bf16[160,128]{1,0:T(8,128)(2,1)}, bf16[160,128]{1,0:T(8,128)(2,1)}, bf16[2048,...) custom-call(bf16[160,2176]{1,0:T(8,128)(2,1)} %get-tuple-element.40.normed.second_in, ...), custom_call_target="tpu_custom_call" | custom-call | tf_op jit(solution)/shard_map/feed_kernel/pallas_call | solution.py:488
  192.1 108.3 %back_kernel.1 = (bf16[160,2048]{1,0:T(8,128)(2,1)}, bf16[160,2048]{1,0:T(8,128)(2,1)}, bf16[2048,128]{1,0:T(8,128)(2,1)}, bf16[1024,128]{1,0:T(8,128)(2,1)}, bf...) custom-call(f32[1,2048]{1,0:T(1,128)} %gain.5, bf16[160,128]{1,0:T(8,128)(2,1)} %get-tuple-element.39.mask, ...), custom_call_target="tpu_custom_call" | custom-call | tf_op jit(solution)/shard_map/back_kernel/pallas_call | solution.py:488
  300.4 7.3 %finish_kernel.1 = (f32[160,2048]{1,0:T(8,128)}, f32[160,2048]{1,0:T(8,128)}, f32[1,2048,128]{2,1,0:T(8,128)}, f32[1,128,768]{2,1,0:T(8,128)}, f32[1,256,128]{2,...) custom-call(bf16[2048,128]{1,0:T(8,128)(2,1)} %get-tuple-element.62., ...), custom_call_target="tpu_custom_call" | custom-call | tf_op jit(solution)/shard_map/finish_kernel/pallas_call | solution.py:1515
